TPU v7x, 128 devices: a whole 4x4x4 slice. The times are simulated.
128 devices in a mesh: lat: 16 (over z, x), lon: 8 (over y, core).
Axes of the slice: x: 4, y: 4, z: 4, core: 2. Of those that a mesh axis runs over, the one named last changes fastest.
Arguments:
- conductivity: bfloat16 [2, 64, 131072], P(None, None, ('lat', 'lon')), may hold values from 0.19921875 to 2
- wind_terms: bfloat16 [4, 64, 131072], P(None, None, ('lat', 'lon')), may hold values from -6 to 6
- correlation_tiles: bfloat16 [1024, 1024, 1024], P(('lat', 'lon')), may hold values from -0.1875 to 0.1875
- tile_targets: int32 [128, 8], P(('lat', 'lon')), may hold values from 0 to 15, as said below
- level_weights: float32 [64], replicated, may hold values from 0.02 to 0.2
- line_levels: int32 [2, 128, 1024], P(None, 'lat', 'lon'), may hold values from 0 to 64, as said below
- potential: float32 [128, 1024], P('lat', 'lon'), may hold values from -6 to 6
Outputs:
- stencil: float32 [9, 128, 1024], P(None, 'lat', 'lon')
- source_term: float32 [128, 1024], P('lat', 'lon')
- geo_field: float32 [2, 131072], P(None, ('lat', 'lon'))
Inputs may be any that keep to these rules, and one draw needn't show every extreme that they name: `tile_targets`: each row holds 8 different apex-latitude block indices. For every magnetic cell line_levels[0] < line_levels[1]; line_levels[0] is below 32.
All inputs are finite; a program needn't handle non-finite values.
Results may differ from a plain program's by a relative error of at most 0.0029.
Values may be sent and summed in bfloat16 or wider, within the bound.
No kernel may reach another device: no remote copies, remote signals or barrier semaphores. Data moves between devices by JAX's collectives and lax.ppermute only.
A program may use at most 128 MiB of HBM per device.

v0:
```python
import jax
import jax.numpy as jnp
from jax import lax
from jax.sharding import PartitionSpec as P

HIGHEST = lax.Precision.HIGHEST


def swapped(block, axis, distance):
    count = lax.axis_size(axis)
    route = []
    for low in range(count):
        high = low | 1 << distance
        if high != low and high < count:
            route += [(low, high), (high, low)]
    return lax.ppermute(block, axis, route)


def with_halo(block, sides, width, periodic):
    for axis, dim in sides:
        count = lax.axis_size(axis)
        forward = [(i, i + 1) for i in range(count - 1)]
        if periodic:
            forward.append((count - 1, 0))
        backward = [(target, source) for source, target in forward]
        low = lax.ppermute(
            lax.slice_in_dim(block, block.shape[dim] - width, None, axis=dim), axis, forward
        )
        high = lax.ppermute(lax.slice_in_dim(block, 0, width, axis=dim), axis, backward)
        block = jnp.concatenate([low, block, high], axis=dim)
    return block


def line_weights(ranges, level_weights):
    levels = jnp.arange(level_weights.shape[0], dtype=jnp.int32)[:, None]
    low_level = jnp.expand_dims(ranges[0], -2)
    high_level = jnp.expand_dims(ranges[1], -2)
    inside = (levels >= low_level) & (levels < high_level)
    return jnp.where(inside, level_weights[:, None], jnp.float32(0.0))


def assemble(extended, row_count, col_count):

    def cells_at(row_step, col_step):
        return extended[
            :, 1 + row_step : 1 + row_step + row_count, 1 + col_step : 1 + col_step + col_count
        ]

    center = cells_at(0, 0)
    eastern = cells_at(0, 1)
    western = cells_at(0, -1)
    northern = cells_at(1, 0)
    southern = cells_at(-1, 0)
    north_east = cells_at(1, 1)
    north_west = cells_at(1, -1)
    south_east = cells_at(-1, 1)
    south_west = cells_at(-1, -1)
    east_coef = 0.5 * (center[0] + eastern[0])
    west_coef = 0.5 * (center[0] + western[0])
    north_coef = 0.5 * (center[0] + northern[0])
    south_coef = 0.5 * (center[0] + southern[0])
    ne_coef = 0.25 * (north_east[1] - center[1])
    nw_coef = -0.25 * (north_west[1] - center[1])
    se_coef = -0.25 * (south_east[1] - center[1])
    sw_coef = 0.25 * (south_west[1] - center[1])
    center_coef = -(
        east_coef + west_coef + north_coef + south_coef + ne_coef + nw_coef + se_coef + sw_coef
    )
    stencil = jnp.stack(
        [
            center_coef,
            east_coef,
            west_coef,
            north_coef,
            south_coef,
            ne_coef,
            nw_coef,
            se_coef,
            sw_coef,
        ]
    )
    zonal_part = eastern[4] - eastern[3] - (western[4] - western[3])
    merid_part = southern[2] + southern[5] - (northern[2] + northern[5])
    source_term = 0.5 * zonal_part + 0.5 * merid_part
    electric = jnp.stack([-0.5 * (eastern[6] - western[6]), -0.5 * (northern[6] - southern[6])])
    return (stencil, source_term, electric)


def per_device(
    conductivity, wind_terms, correlation_tiles, tile_targets, level_weights, line_levels, potential
):
    n_lat = lax.axis_size("lat")
    fields = jnp.concatenate([conductivity, wind_terms], 0)
    planes = fields.shape[0]
    levels_n = fields.shape[1]
    geo_cells = fields.shape[2]
    mag_cells = correlation_tiles.shape[1]
    rows_mag = potential.shape[0]
    cols_mag = potential.shape[1]
    targets = tile_targets[0]
    flat_fields = fields.reshape(planes * levels_n, geo_cells)
    partial_value = lax.dot_general(
        flat_fields, correlation_tiles, (((1,), (2,)), ((), ())), preferred_element_type=jnp.float32
    )
    block_rows = planes * levels_n
    wanted = jnp.arange(block_rows * lax.axis_size("lat") // block_rows, dtype=jnp.int32)[None, :]
    selector = (targets[:, None] == wanted).astype(jnp.float32)
    block_sum = jnp.einsum("kb,fkc->bfc", selector, partial_value, precision=HIGHEST)
    regridded = lax.psum_scatter(
        block_sum.reshape(block_rows * lax.axis_size("lat"), mag_cells),
        "lat",
        scatter_dimension=0,
        tiled=True,
    )
    weights = line_weights(line_levels.reshape(2, mag_cells), level_weights)
    integrated = jnp.einsum(
        "flc,lc->fc", regridded.reshape(planes, levels_n, mag_cells), weights, precision=HIGHEST
    )
    mag_grid = integrated.reshape(planes, rows_mag, cols_mag)
    mirrored = mag_grid
    for bit_index in range(n_lat.bit_length() - 1):
        mirrored = swapped(mirrored, "lat", bit_index)
    mirrored = mirrored[:, ::-1, :]
    combined = mag_grid + mirrored
    stacked = jnp.concatenate([combined, potential[None]], 0)
    widened = with_halo(stacked, (("lon", 2),), 1, True)
    extended = with_halo(widened, (("lat", 1),), 1, False)
    stencil, source_term, electric = assemble(extended, rows_mag, cols_mag)
    electric_flat = electric.astype(jnp.bfloat16).reshape(2, mag_cells)
    every_field = lax.all_gather(electric_flat[None], "lat", axis=0, tiled=True)
    chosen = jnp.take(every_field, targets, axis=0)
    geo_field = lax.dot_general(
        chosen, correlation_tiles, (((0, 2), (0, 1)), ((), ())), preferred_element_type=jnp.float32
    )
    return (stencil, source_term, geo_field)


def solution(mesh):
    in_specs = (
        P(None, None, ("lat", "lon")),
        P(None, None, ("lat", "lon")),
        P(("lat", "lon"), None, None),
        P(("lat", "lon"), None),
        P(),
        P(None, "lat", "lon"),
        P("lat", "lon"),
    )
    out_specs = (P(None, "lat", "lon"), P("lat", "lon"), P(None, ("lat", "lon")))
    return jax.shard_map(
        per_device, mesh=mesh, in_specs=in_specs, out_specs=out_specs, check_vma=False
    )
```

profile of v0, /device:TPU:0, one launch (start us, length us, event | category | flops | bytes accessed | tf_op | source)
XLA Modules:
  0.0 302.8 jit_solution(14283408824015323627)
XLA Ops:
  7.2 0.0 reduce-scatter.2.cloned.1.call-start
  7.2 1.2 pad_maximum_fusion
  8.4 13.0 %fusion.36 = f32[384,8,1024]{2,0,1:T(8,128)} fusion(bf16[384,1024,1]{1,0,2:T(8,128)(2,1)S(1)} %bitcast.39, bf16[8,1024,1024]{2,1,0:T(8,128)(2,1)} %param.9), kind=kOutput, calls=%fused_computation.83 | convolution fusion | flops 6442450944 | bytes 30146560 | tf_op jit(solution)/shard_map/dot_general | solution.py:102
  21.4 20.6 %fusion = f32[16,384,1024]{2,0,1:T(8,128)S(1)} fusion(f32[384,8,1024]{2,0,1:T(8,128)} %fusion.36, s32[8]{0:T(128)S(1)} %bitcast.48), kind=kOutput, calls=%fused_computation.1 | convolution fusion | flops 603979904 | bytes 37748768 | tf_op jit(solution)/shard_map/kb,fkc->bfc/dot_general | solution.py:108
  42.0 28.6 %copy.12 = f32[16,384,1024]{2,1,0:T(8,128)} copy(f32[16,384,1024]{2,0,1:T(8,128)S(1)} %fusion) | data formatting | bytes 50331648 | tf_op jit(solution)/shard_map/kb,fkc->bfc/dot_general | solution.py:108
  70.6 0.0 reduce-scatter.2.cloned.1.call-update
  70.6 0.7 copy-done.1
  71.3 0.1 select_bitcast_fusion
  71.4 155.1 %reduce-scatter.2.cloned.1.call-done = f32[384,1024]{1,0:T(8,128)} async-done(((f32[6144,1024]{1,0:T(8,128)}), f32[384,1024]{1,0:T(8,128)}) %reduce-scatter.2.cloned.1.call-update) | async-done | bytes 1572880 | tf_op jit(solution)/shard_map/reduce_scatter | solution.py:109
  226.5 1.6 multiply_reduce_fusion
  228.1 1.6 collective-permute-start
  229.7 2.3 collective-permute-done
  232.0 3.0 collective-permute-start.1
  235.0 2.3 collective-permute-done.1
  237.4 1.3 collective-permute-start.2
  238.7 2.5 collective-permute-done.2
  241.2 3.0 collective-permute-start.3
  244.2 2.4 collective-permute-done.3
  246.6 0.1 slice_maximum_fusion
  246.6 3.0 collective-permute-start.4
  249.6 1.5 collective-permute-done.5
  251.1 0.0 collective-permute-done.4
  251.2 0.1 pad_maximum_fusion.2
  251.3 1.3 collective-permute-start.6
  252.6 4.6 %collective-permute-start.7 = (f32[7,1,130]{2,1,0:T(1,128)S(1)}, f32[7,1,130]{2,1,0:T(1,128)S(1)}, u32[]{:S(2)}, u32[]{:S(2)}) collective-permute-start(f32[7,1,130]{2,1,0:T(1,128)S(1)} %get-tuple-element.14), channel_id=1, source_target_pairs={{0,8},{8,16},{16,24},{24,32},{32,40},{40,48},{48,56},{56,64},{64,7... | collective-permute-start | bytes 10928 | tf_op jit(solution)/shard_map/ppermute | solution.py:26
  257.2 1.3 collective-permute-done.7
  258.5 0.1 fusion.9
  258.6 27.1 %all_gather.3 = bf16[16,2,1024]{2,1,0:T(2,128)(2,1)S(1)} all-gather(bf16[1,2,1024]{2,1,0:T(2,128)(2,1)S(1)} %pad_maximum_fusion.18), channel_id=1, replica_groups=mesh['lat'=16,'lon'=8] {'lat'}, dimensions={0}, use_global_device_ids=true | all-gather | bytes 69632 | tf_op jit(solution)/shard_map/all_gather | solution.py:130
  285.8 0.1 constant_dynamic-update-slice_fusion.8
  285.9 0.6 gather_fusion
  286.6 8.7 %convolution_bitcast_fusion = f32[2,1024]{1,0:T(2,128)} fusion(bf16[8,1024,1024]{2,1,0:T(8,128)(2,1)} %param.9, bf16[8,2,1024]{2,1,0:T(2,128)(2,1)S(1)} %gather_fusion, pred[8]{0:T(512)(128)(4,1)S(1)} %compare_and_fusion), kind=kOutput, calls=%fused_computation.4 | convolution fusion | flops 33570816 | bytes 16818184 | tf_op jit(solution)/shard_map/dot_general | solution.py:132
  295.3 0.7 fusion.13
  (29 shorter events, 0.1 us)
Async XLA Ops:
  7.2 219.3 %reduce-scatter.2.cloned.1.call-start = ((), (), s32[]{:S(2)}) async-start(), calls=%async_computation.1 | async-start | bytes 26738688 | tf_op jit(solution)/shard_map/reduce_scatter | solution.py:109
  8.4 13.0 %copy-start.3 = (s32[1,8]{1,0:T(1,128)S(1)}, s32[1,8]{1,0:T(1,128)}, u32[]{:S(2)}) copy-start(s32[1,8]{1,0:T(1,128)} %param.10) | copy-start | bytes 100
  70.6 0.7 copy-start.1
  70.6 0.7 copy-start.2
  70.6 176.0 %copy-start = (f32[8,128]{1,0:T(8,128)S(1)}, f32[8,128]{1,0:T(8,128)}, u32[]{:S(2)}) copy-start(f32[8,128]{1,0:T(8,128)} %param.13) | copy-start | bytes 12292
  228.1 3.9 %collective-permute-start = (f32[6,8,128]{2,1,0:T(8,128)S(1)}, f32[6,8,128]{2,1,0:T(8,128)S(1)}, u32[]{:S(2)}, u32[]{:S(2)}) collective-permute-start(f32[6,8,128]{2,1,0:T(8,128)S(1)} %bitcast.47), channel_id=1, source_target_pairs={{0,8},{8,0},{16,24},{24,16},{32,40},{40,32},{48,56},{56,48},{64,72... | collective-permute-start | bytes 73736 | tf_op jit(solution)/shard_map/ppermute | solution.py:16
  232.0 5.3 %collective-permute-start.1 = (f32[6,8,128]{2,1,0:T(8,128)S(1)}, f32[6,8,128]{2,1,0:T(8,128)S(1)}, u32[]{:S(2)}, u32[]{:S(2)}) collective-permute-start(f32[6,8,128]{2,1,0:T(8,128)S(1)} %collective-permute-done), channel_id=1, source_target_pairs={{0,16},{16,0},{8,24},{24,8},{32,48},{48,32},{40,56},{56,40},{64,80... | collective-permute-start | bytes 73736 | tf_op jit(solution)/shard_map/ppermute | solution.py:16
  237.4 3.8 %collective-permute-start.2 = (f32[6,8,128]{2,1,0:T(8,128)S(1)}, f32[6,8,128]{2,1,0:T(8,128)S(1)}, u32[]{:S(2)}, u32[]{:S(2)}) collective-permute-start(f32[6,8,128]{2,1,0:T(8,128)S(1)} %collective-permute-done.1), channel_id=1, source_target_pairs={{0,32},{32,0},{8,40},{40,8},{16,48},{48,16},{24,56},{56,24},{64,96... | collective-permute-start | bytes 73736 | tf_op jit(solution)/shard_map/ppermute | solution.py:16
  241.2 5.3 %collective-permute-start.3 = (f32[6,8,128]{2,1,0:T(8,128)S(1)}, f32[6,8,128]{2,1,0:T(8,128)S(1)}, u32[]{:S(2)}, u32[]{:S(2)}) collective-permute-start(f32[6,8,128]{2,1,0:T(8,128)S(1)} %collective-permute-done.2), channel_id=1, source_target_pairs={{0,64},{64,0},{8,72},{72,8},{16,80},{80,16},{24,88},{88,24},{32,96... | collective-permute-start | bytes 73736 | tf_op jit(solution)/shard_map/ppermute | solution.py:16
  246.6 4.5 %collective-permute-start.5 = (f32[7,8,1]{2,1,0:T(8,128)S(1)}, f32[7,8,1]{2,1,0:T(8,128)S(1)}, u32[]{:S(2)}, u32[]{:S(2)}) collective-permute-start(f32[7,8,1]{2,1,0:T(8,128)S(1)} %get-tuple-element.17), channel_id=1, source_target_pairs={{0,1},{1,2},{2,3},{3,4},{4,5},{5,6},{6,7},{7,0},{8,9},{9,10},{10,1... | collective-permute-start | bytes 680 | tf_op jit(solution)/shard_map/ppermute | solution.py:26
  246.6 4.5 %collective-permute-start.4 = (f32[7,8,1]{2,1,0:T(8,128)S(1)}, f32[7,8,1]{2,1,0:T(8,128)S(1)}, u32[]{:S(2)}, u32[]{:S(2)}) collective-permute-start(f32[7,8,1]{2,1,0:T(8,128)S(1)} %get-tuple-element.16), channel_id=1, source_target_pairs={{1,0},{2,1},{3,2},{4,3},{5,4},{6,5},{7,6},{0,7},{9,8},{10,9},{11,1... | collective-permute-start | bytes 680 | tf_op jit(solution)/shard_map/ppermute | solution.py:29
  251.3 5.9 %collective-permute-start.6 = (f32[7,1,130]{2,1,0:T(1,128)S(1)}, f32[7,1,130]{2,1,0:T(1,128)S(1)}, u32[]{:S(2)}, u32[]{:S(2)}) collective-permute-start(f32[7,1,130]{2,1,0:T(1,128)S(1)} %get-tuple-element.15), channel_id=1, source_target_pairs={{8,0},{16,8},{24,16},{32,24},{40,32},{48,40},{56,48},{64,56},{72,6... | collective-permute-start | bytes 10928 | tf_op jit(solution)/shard_map/ppermute | solution.py:29
  252.6 5.9 %collective-permute-start.7 = (f32[7,1,130]{2,1,0:T(1,128)S(1)}, f32[7,1,130]{2,1,0:T(1,128)S(1)}, u32[]{:S(2)}, u32[]{:S(2)}) collective-permute-start(f32[7,1,130]{2,1,0:T(1,128)S(1)} %get-tuple-element.14), channel_id=1, source_target_pairs={{0,8},{8,16},{16,24},{24,32},{32,40},{40,48},{48,56},{56,64},{64,7... | collective-permute-start | bytes 10928 | tf_op jit(solution)/shard_map/ppermute | solution.py:26
  285.9 10.0 %copy-start.4 = (f32[9,8,128]{2,1,0:T(8,128)}, f32[9,8,128]{2,1,0:T(8,128)S(1)}, u32[]{:S(2)}) copy-start(f32[9,8,128]{2,1,0:T(8,128)S(1)} %constant_dynamic-update-slice_fusion) | copy-start | bytes 110596
Sparse Core Ops, SparseCore 0:
  70.7 155.6 reduce-scatter.1
where the time goes:
time: 303 us
  waiting for transfers between devices  167 us (55%)
  matrix products  42.3 us (14%)
  local copies, waits for them, and re-layouts  30 us (10%)
  blocking collectives  27.1 us (9%)
  starting transfers between devices  17.7 us (6%)
  between operations  14.2 us (5%)
  other arithmetic  4.01 us (1%)
    reduce_scatter x1, waiting for transfers between devices, per_device(): lax.psum_scatter(block_sum.reshape(block_rows * lax.axis_size('lat'), mag...  155 us
    dot_general x1, local copies, waits for them, and re-layouts, per_device(): jnp.einsum('kb,fkc->bfc', selector, partial_value, precision=HIGHEST)  28.6 us
    all_gather x1, blocking collectives, per_device(): every_field = lax.all_gather(electric_flat[None], 'lat', axis=0, tiled=True)  27.1 us
    dot_general x1, matrix products, per_device(): jnp.einsum('kb,fkc->bfc', selector, partial_value, precision=HIGHEST)  20.6 us
    dot_general x1, matrix products, per_device(): lax.dot_general(flat_fields, correlation_tiles, (((1,), (2,)), ((), ())),...  13 us
    ppermute x4, waiting for transfers between devices, swapped(): return lax.ppermute(block, axis, route)  9.56 us
    ppermute x4, starting transfers between devices, swapped(): return lax.ppermute(block, axis, route)  8.83 us
    dot_general x1, matrix products, per_device(): lax.dot_general(chosen, correlation_tiles, (((0, 2), (0, 1)), ((), ())),...  8.69 us
  transfers between devices with their start and end apart: 9, of which 7 were waited for; matrix products, arithmetic and copies ran while one was open for 0% of the time, Pallas kernels for 0%

commit v1 on v0

v1 whole, which is shorter than its diff:
```python
import functools

import jax
import jax.numpy as jnp
from jax import lax
from jax.experimental import pallas as pl
from jax.experimental.pallas import tpu as pltpu
from jax.sharding import PartitionSpec as P

RADIX = 128.0
ROWS, COLS = 8, 128
SUM_ROWS = 40


def pack_kernel(levels_ref, potential_ref, out_ref):
    packed = levels_ref[0].astype(jnp.float32) * RADIX + levels_ref[1].astype(jnp.float32)
    potential = potential_ref[...]
    for target in range(out_ref.shape[0]):
        out_ref[target, 0:ROWS, :] = packed
        out_ref[target, ROWS : 2 * ROWS, :] = potential


def pack(line_levels, potential, n_lat):
    return pl.pallas_call(
        pack_kernel,
        out_shape=jax.ShapeDtypeStruct((n_lat, 2 * ROWS, COLS), jnp.float32),
        in_specs=[pl.BlockSpec(memory_space=pltpu.VMEM)] * 2,
        out_specs=pl.BlockSpec(memory_space=pltpu.VMEM),
        name="pack_levels_potential",
    )(line_levels, potential)


def row_above(block, edge):
    rows = lax.broadcasted_iota(jnp.int32, block.shape, 0)
    return jnp.where(rows == ROWS - 1, edge, pltpu.roll(block, ROWS - 1, 0))


def row_below(block, edge):
    rows = lax.broadcasted_iota(jnp.int32, block.shape, 0)
    return jnp.where(rows == 0, edge, pltpu.roll(block, 1, 0))


def forward_kernel(
    targets, level_weights, conductivity, wind, gathered, tiles_hbm, out_ref, tiles, fields, weights, plain, mirrored, sems
):
    tile_count, mag_cells, geo_cells = tiles.shape
    levels_n = conductivity.shape[1]
    n_lat = gathered.shape[0]
    copies = [
        pltpu.make_async_copy(tiles_hbm.at[k], tiles.at[k], sems.at[k]) for k in range(tile_count)
    ]
    for copy in copies:
        copy.start()

    for level in range(levels_n):
        weights[level : level + 1, :] = jnp.full((1, COLS), level_weights[level], jnp.float32)
    fields[0:levels_n, :] = conductivity[0]
    fields[levels_n : 2 * levels_n, :] = conductivity[1]
    first, second, third, fourth = (wind[i].astype(jnp.float32) for i in range(4))
    fields[2 * levels_n : 3 * levels_n, :] = (third - second).astype(jnp.bfloat16)
    fields[3 * levels_n : 4 * levels_n, :] = (first + fourth).astype(jnp.bfloat16)
    plain[...] = jnp.zeros_like(plain)
    mirrored[...] = jnp.zeros_like(mirrored)
    level_of = lax.broadcasted_iota(jnp.int32, (levels_n, COLS), 0).astype(jnp.float32)

    chunk = 2 * COLS
    for k in range(tile_count):
        copies[k].wait()
        target = targets[0, k]
        opposite = n_lat - 1 - target
        for start in range(0, mag_cells, chunk):
            partial_value = lax.dot_general(
                fields[...],
                tiles[k, start : start + chunk, :],
                (((1,), (1,)), ((), ())),
                preferred_element_type=jnp.float32,
            )
            for piece in range(chunk // COLS):
                row = start // COLS + piece
                bounds = gathered[target, row : row + 1, :]
                low = jnp.floor(bounds * (1.0 / RADIX))
                high = bounds - low * RADIX
                inside = (level_of >= low) & (level_of < high)
                weight = jnp.where(inside, weights[...], 0.0)
                for f in range(4):
                    part = partial_value[
                        f * levels_n : (f + 1) * levels_n, piece * COLS : (piece + 1) * COLS
                    ]
                    total = jnp.sum(part * weight, axis=0, keepdims=True)
                    plain[target, f, row : row + 1, :] = total
                    mirrored[opposite, f, ROWS - 1 - row : ROWS - row, :] = total

    combined = [[plain[b, f] + mirrored[b, f] for f in range(4)] for b in range(n_lat)]
    nothing = jnp.zeros((1, COLS), jnp.float32)
    for b in range(n_lat):
        def edges(f):
            above = combined[b + 1][f][0:1] if b + 1 < n_lat else nothing
            below = combined[b - 1][f][ROWS - 1 : ROWS] if b > 0 else nothing
            return below, above

        merid = combined[b][3]
        below, above = edges(3)
        out_ref[b, 0:8, :] = combined[b][0]
        out_ref[b, 8:16, :] = combined[b][1]
        out_ref[b, 16:24, :] = combined[b][2]
        out_ref[b, 24:32, :] = row_below(merid, below) - row_above(merid, above)
        below0, above0 = edges(0)
        below1, above1 = edges(1)
        out_ref[b, 32:33, :] = below0
        out_ref[b, 33:34, :] = above0
        out_ref[b, 34:35, :] = below1
        out_ref[b, 35:36, :] = above1
        out_ref[b, 36:40, :] = jnp.zeros((4, COLS), jnp.float32)


def forward(targets, level_weights, conductivity, wind, gathered, tiles):
    n_lat = gathered.shape[0]
    levels_n, geo_cells = conductivity.shape[1:]
    smem = pl.BlockSpec(memory_space=pltpu.SMEM)
    vmem = pl.BlockSpec(memory_space=pltpu.VMEM)
    return pl.pallas_call(
        forward_kernel,
        out_shape=(
            jax.ShapeDtypeStruct((n_lat, SUM_ROWS, COLS), jnp.float32),
            pltpu.VMEM(tiles.shape, tiles.dtype),
        ),
        in_specs=[smem, smem, vmem, vmem, vmem, pl.BlockSpec(memory_space=pl.ANY)],
        out_specs=(vmem, vmem),
        scratch_shapes=[
            pltpu.VMEM((4 * levels_n, geo_cells), jnp.bfloat16),
            pltpu.VMEM((levels_n, COLS), jnp.float32),
            pltpu.VMEM((n_lat, 4, ROWS, COLS), jnp.float32),
            pltpu.VMEM((n_lat, 4, ROWS, COLS), jnp.float32),
            pltpu.SemaphoreType.DMA((tiles.shape[0],)),
        ],
        compiler_params=pltpu.CompilerParams(vmem_limit_bytes=40 * 2**20),
        cost_estimate=pl.CostEstimate(
            flops=2 * 4 * levels_n * tiles.size, bytes_accessed=2 * tiles.size, transcendentals=0
        ),
        name="regrid_integrate",
    )(targets, level_weights, conductivity, wind, gathered, tiles)


def backward_kernel(targets, gathered, west, east, tiles, out_ref, zonal, merid, rows_ref):
    tile_count, mag_cells, geo_cells = tiles.shape
    n_lat = gathered.shape[0]
    lanes = lax.broadcasted_iota(jnp.int32, (ROWS, COLS), 1)
    nothing = jnp.zeros((1, COLS), jnp.float32)
    for b in range(n_lat):
        here = gathered[b, ROWS : 2 * ROWS, :]
        eastern = jnp.where(
            lanes == COLS - 1, pltpu.roll(east[b, ROWS : 2 * ROWS, :], COLS - 1, 1), pltpu.roll(here, COLS - 1, 1)
        )
        western = jnp.where(
            lanes == 0, pltpu.roll(west[b, ROWS : 2 * ROWS, :], 1, 1), pltpu.roll(here, 1, 1)
        )
        above = gathered[b + 1, ROWS : ROWS + 1, :] if b + 1 < n_lat else nothing
        below = gathered[b - 1, 2 * ROWS - 1 : 2 * ROWS, :] if b > 0 else nothing
        zonal[b] = -0.5 * (eastern - western)
        merid[b] = -0.5 * (row_above(here, above) - row_below(here, below))
    rows_ref[...] = jnp.zeros_like(rows_ref)
    total = jnp.zeros((ROWS, geo_cells), jnp.float32)
    for k in range(tile_count):
        target = targets[0, k]
        for row in range(ROWS):
            columns = slice(row * COLS, (row + 1) * COLS)
            rows_ref[k, 0:1, columns] = zonal[target, row : row + 1, :]
            rows_ref[k, 1:2, columns] = merid[target, row : row + 1, :]
        total += jnp.dot(
            rows_ref[k].astype(jnp.bfloat16), tiles[k], preferred_element_type=jnp.float32
        )
    out_ref[...] = total[0:2]


def backward(targets, gathered, west, east, tiles):
    n_lat = gathered.shape[0]
    tile_count, mag_cells, geo_cells = tiles.shape
    smem = pl.BlockSpec(memory_space=pltpu.SMEM)
    vmem = pl.BlockSpec(memory_space=pltpu.VMEM)
    return pl.pallas_call(
        backward_kernel,
        out_shape=jax.ShapeDtypeStruct((2, geo_cells), jnp.float32),
        in_specs=[smem, vmem, vmem, vmem, vmem],
        out_specs=vmem,
        scratch_shapes=[
            pltpu.VMEM((n_lat, ROWS, COLS), jnp.float32),
            pltpu.VMEM((n_lat, ROWS, COLS), jnp.float32),
            pltpu.VMEM((tile_count, ROWS, mag_cells), jnp.float32),
        ],
        compiler_params=pltpu.CompilerParams(vmem_limit_bytes=40 * 2**20),
        cost_estimate=pl.CostEstimate(
            flops=16 * tiles.size, bytes_accessed=2 * tiles.size, transcendentals=0
        ),
        name="electric_to_geo",
    )(targets, gathered, west, east, tiles)


def stencil_kernel(sums, west, east, stencil_ref, source_ref):
    lanes = lax.broadcasted_iota(jnp.int32, (ROWS, COLS), 1)

    def eastward(begin):
        return jnp.where(
            lanes == COLS - 1,
            pltpu.roll(east[begin : begin + ROWS, :], COLS - 1, 1),
            pltpu.roll(sums[begin : begin + ROWS, :], COLS - 1, 1),
        )

    def westward(begin):
        return jnp.where(
            lanes == 0,
            pltpu.roll(west[begin : begin + ROWS, :], 1, 1),
            pltpu.roll(sums[begin : begin + ROWS, :], 1, 1),
        )

    edge, edge_east, edge_west = sums[32:40, :], eastward(32), westward(32)
    center0, center1 = sums[0:8, :], sums[8:16, :]
    east1, west1 = eastward(8), westward(8)
    east_coef = 0.5 * (center0 + eastward(0))
    west_coef = 0.5 * (center0 + westward(0))
    north_coef = 0.5 * (center0 + row_above(center0, edge[1:2]))
    south_coef = 0.5 * (center0 + row_below(center0, edge[0:1]))
    ne_coef = 0.25 * (row_above(east1, edge_east[3:4]) - center1)
    nw_coef = -0.25 * (row_above(west1, edge_west[3:4]) - center1)
    se_coef = -0.25 * (row_below(east1, edge_east[2:3]) - center1)
    sw_coef = 0.25 * (row_below(west1, edge_west[2:3]) - center1)
    others = [east_coef, west_coef, north_coef, south_coef, ne_coef, nw_coef, se_coef, sw_coef]
    stencil_ref[0] = -sum(others[1:], others[0])
    for i, coef in enumerate(others):
        stencil_ref[i + 1] = coef
    source_ref[...] = 0.5 * (eastward(16) - westward(16)) + 0.5 * sums[24:32, :]


def stencil_source(sums, west, east):
    vmem = pl.BlockSpec(memory_space=pltpu.VMEM)
    return pl.pallas_call(
        stencil_kernel,
        out_shape=(
            jax.ShapeDtypeStruct((9, ROWS, COLS), jnp.float32),
            jax.ShapeDtypeStruct((ROWS, COLS), jnp.float32),
        ),
        in_specs=[vmem] * 3,
        out_specs=(vmem, vmem),
        name="stencil_source",
    )(sums, west, east)


def lon_neighbours(block):
    count = lax.axis_size("lon")
    from_west = [(i, (i + 1) % count) for i in range(count)]
    from_east = [((i + 1) % count, i) for i in range(count)]
    return lax.ppermute(block, "lon", from_west), lax.ppermute(block, "lon", from_east)


def per_device(
    conductivity, wind_terms, correlation_tiles, tile_targets, level_weights, line_levels, potential
):
    n_lat = lax.axis_size("lat")
    packed = pack(line_levels, potential, n_lat)
    gathered = lax.all_to_all(packed, "lat", 0, 0, tiled=True)
    west, east = lon_neighbours(gathered)
    sends, tiles = forward(
        tile_targets, level_weights, conductivity, wind_terms, gathered, correlation_tiles
    )
    received = lax.all_to_all(sends, "lat", 0, 0, tiled=True)
    sums = jnp.sum(received, axis=0)
    sums_west, sums_east = lon_neighbours(sums)
    geo_field = backward(tile_targets, gathered, west, east, tiles)
    stencil, source_term = stencil_source(sums, sums_west, sums_east)
    return stencil, source_term, geo_field


def solution(mesh):
    in_specs = (
        P(None, None, ("lat", "lon")),
        P(None, None, ("lat", "lon")),
        P(("lat", "lon"), None, None),
        P(("lat", "lon"), None),
        P(),
        P(None, "lat", "lon"),
        P("lat", "lon"),
    )
    out_specs = (P(None, "lat", "lon"), P("lat", "lon"), P(None, ("lat", "lon")))
    return jax.shard_map(
        per_device, mesh=mesh, in_specs=in_specs, out_specs=out_specs, check_vma=False
    )
```

time: 303 us -> 60.7 us (0.20)
  the two profiles are of different devices: /device:TPU:0 before, /device:TPU:1 now
where the time goes in v1:
time: 60.7 us; the launch traced here: 60.2 us
  Pallas kernels  21.3 us (35%)
  blocking collectives  15.4 us (25%)
  starting transfers between devices  11.2 us (18%)
  local copies, waits for them, and re-layouts  6.94 us (11%)
  waiting for transfers between devices  4.66 us (8%)
  between operations  0.7 us (1%)
    all_to_all x1, blocking collectives, per_device(): gathered = lax.all_to_all(packed, 'lat', 0, 0, tiled=True)  15.4 us
    pallas_call x1, Pallas kernels, forward(): pl.pallas_call(forward_kernel, out_shape=(jax.ShapeDtypeStruct((n_lat, SU...  9.75 us
    pallas_call x1, Pallas kernels, backward(): pl.pallas_call(backward_kernel, out_shape=jax.ShapeDtypeStruct((2, geo_ce...  8.77 us
    unnamed x12, local copies, waits for them, and re-layouts  6.94 us
    ppermute x2, starting transfers between devices, lon_neighbours(): lax.ppermute(block, 'lon', from_east)  5.2 us
    all_to_all x1, waiting for transfers between devices, per_device(): received = lax.all_to_all(sends, 'lat', 0, 0, tiled=True)  4.65 us
    all_to_all x1, starting transfers between devices, per_device(): received = lax.all_to_all(sends, 'lat', 0, 0, tiled=True)  3.54 us
    ppermute x2, starting transfers between devices, lon_neighbours(): lax.ppermute(block, 'lon', from_west)  2.42 us
  transfers between devices with their start and end apart: 5, of which 1 were waited for; matrix products, arithmetic and copies ran while one was open for 0% of the time, Pallas kernels for 15%

profile of v1, /device:TPU:1, one launch (start us, length us, event | category | flops | bytes accessed | tf_op | source)
XLA Modules:
  0.0 60.2 jit_solution(15280626588073849932)
XLA Ops:
  0.6 0.0 copy-start.2
  0.6 1.4 %pack_levels_potential.1 = f32[16,16,128]{2,1,0:T(8,128)} custom-call(s32[2,8,128]{2,1,0:T(8,128)} %levels_ref.1, f32[8,128]{1,0:T(8,128)} %potential_ref.1), custom_call_target="tpu_custom_call" | custom-call | tf_op jit(solution)/shard_map/pack_levels_potential/pallas_call | solution.py:24
  2.0 15.4 %all_to_all.10.gathered = f32[16,16,128]{2,1,0:T(8,128)} all-to-all(f32[16,16,128]{2,1,0:T(8,128)} %pack_levels_potential.1), channel_id=1, replica_groups=mesh['lat'=16,'lon'=8] {'lat'}, dimensions={0} | all-to-all | bytes 262144 | tf_op jit(solution)/shard_map/all_to_all | solution.py:259
  17.4 0.0 copy-start.1
  17.4 9.7 %regrid_integrate.1 = (f32[16,40,128]{2,1,0:T(8,128)}, bf16[8,1024,1024]{2,1,0:T(8,128)(2,1)S(1)}) custom-call(s32[1,8]{1,0:T(1,128)} %targets.3, f32[64]{0:T(128)} %level_weights.1, bf16[2,64,1024]{2,1,0:T(8,128)(2,1)} %conductivity.1, bf16[4,64,1024]{2,1,0:T(8,128)(2,1)} %wind.1, f32[16,16,128]{2,1,0:T(8,128)} %all_to_all.10.gathered, ...), custom_call_target="tpu_custom_call" | custom-call | flops 4294967296 | bytes 16777216 | tf_op jit(solution)/shard_map/regrid_integrate/pallas_call | solution.py:121
  27.2 0.0 copy-start
  27.2 5.7 %copy-done = bf16[8,1024,1024]{2,1,0:T(8,128)(2,1)} copy-done((bf16[8,1024,1024]{2,1,0:T(8,128)(2,1)}, bf16[8,1024,1024]{2,1,0:T(8,128)(2,1)S(1)}, u32[]{:S(2)}) %copy-start) | copy-done | bytes 16777240
  32.9 3.5 %all-to-all-start.1 = ((f32[16,40,128]{2,1,0:T(8,128)}), f32[16,40,128]{2,1,0:T(8,128)S(1)}, u32[]{:S(2)}, u32[]{:S(2)}) async-start(f32[16,40,128]{2,1,0:T(8,128)} %get-tuple-element.7), calls=%async_computation.1 | async-start | bytes 655360 | tf_op jit(solution)/shard_map/all_to_all | solution.py:264
  36.4 0.0 copy-done.1
  36.5 2.1 %collective-permute-start.3 = (f32[16,16,128]{2,1,0:T(8,128)S(1)}, f32[16,16,128]{2,1,0:T(8,128)S(1)}, u32[]{:S(2)}, u32[]{:S(2)}) collective-permute-start(f32[16,16,128]{2,1,0:T(8,128)S(1)} %copy-done.1), channel_id=1, source_target_pairs={{1,0},{2,1},{3,2},{4,3},{5,4},{6,5},{7,6},{0,7},{9,8},{10,9},{11,1... | collective-permute-start | bytes 393224 | tf_op jit(solution)/shard_map/ppermute | solution.py:251
  38.5 1.2 %collective-permute-start.2 = (f32[16,16,128]{2,1,0:T(8,128)S(1)}, f32[16,16,128]{2,1,0:T(8,128)S(1)}, u32[]{:S(2)}, u32[]{:S(2)}) collective-permute-start(f32[16,16,128]{2,1,0:T(8,128)S(1)} %copy-done.1), channel_id=1, source_target_pairs={{0,1},{1,2},{2,3},{3,4},{4,5},{5,6},{6,7},{7,0},{8,9},{9,10},{10,1... | collective-permute-start | bytes 393224 | tf_op jit(solution)/shard_map/ppermute | solution.py:251
  39.7 4.7 %all-to-all-done.1 = f32[16,40,128]{2,1,0:T(8,128)S(1)} async-done(((f32[16,40,128]{2,1,0:T(8,128)}), f32[16,40,128]{2,1,0:T(8,128)S(1)}, u32[]{:S(2)}, u32[]{:S(2)}) %all-to-all-start.1) | async-done | bytes 327712 | tf_op jit(solution)/shard_map/all_to_all | solution.py:264
  44.4 0.0 copy-start.3
  44.4 3.1 %collective-permute-start.1 = (f32[40,128]{1,0:T(8,128)S(1)}, f32[40,128]{1,0:T(8,128)S(1)}, u32[]{:S(2)}, u32[]{:S(2)}) collective-permute-start(f32[40,128]{1,0:T(8,128)S(1)} %reduce_sum.9.sums), channel_id=1, source_target_pairs={{1,0},{2,1},{3,2},{4,3},{5,4},{6,5},{7,6},{0,7},{9,8},{10,9},{11,1... | collective-permute-start | bytes 61448 | tf_op jit(solution)/shard_map/ppermute | solution.py:251
  47.6 1.2 %collective-permute-start = (f32[40,128]{1,0:T(8,128)S(1)}, f32[40,128]{1,0:T(8,128)S(1)}, u32[]{:S(2)}, u32[]{:S(2)}) collective-permute-start(f32[40,128]{1,0:T(8,128)S(1)} %reduce_sum.9.sums), channel_id=1, source_target_pairs={{0,1},{1,2},{2,3},{3,4},{4,5},{5,6},{6,7},{7,0},{8,9},{9,10},{10,1... | collective-permute-start | bytes 61448 | tf_op jit(solution)/shard_map/ppermute | solution.py:251
  48.8 0.0 collective-permute-done.3.east
  48.8 0.0 collective-permute-done.2.west
  48.8 0.0 copy-done.2
  48.8 8.8 %electric_to_geo.1 = f32[2,1024]{1,0:T(2,128)} custom-call(s32[1,8]{1,0:T(1,128)S(1)} %copy-done.2, f32[16,16,128]{2,1,0:T(8,128)S(1)} %copy-done.1, f32[16,16,128]{2,1,0:T(8,128)S(1)} %collective-permute-done.2.west, f32[16,16,128]{2,1,0:T(8,128)S(1)} %collective-permute-done.3.east, bf16[8,1024,1024]{2,1,0:T(8,128)(2,1)} %copy-done), custom_call_target="tpu_custom_call" | custom-call | flops 134217728 | bytes 16777216 | tf_op jit(solution)/shard_map/electric_to_geo/pallas_call | solution.py:180
  57.6 0.0 collective-permute-done.1.east
  57.6 0.0 copy-start.4
  57.6 0.0 collective-permute-done.west
  57.6 0.0 copy-done.3
  57.6 0.6 copy-done.4
  58.2 0.0 copy-start.5
  58.2 0.6 copy-done.5
  58.8 1.5 %stencil_source.1 = (f32[9,8,128]{2,1,0:T(8,128)}, f32[8,128]{1,0:T(8,128)}) custom-call(f32[40,128]{1,0:T(8,128)} %copy-done.3, f32[40,128]{1,0:T(8,128)} %copy-done.5, f32[40,128]{1,0:T(8,128)} %copy-done.4), custom_call_target="tpu_custom_call" | custom-call | tf_op jit(solution)/shard_map/stencil_source/pallas_call | solution.py:235
  (1 shorter events, 0.0 us)
Async XLA Ops:
  0.6 48.2 %copy-start.2 = (s32[1,8]{1,0:T(1,128)S(1)}, s32[1,8]{1,0:T(1,128)}, u32[]{:S(2)}) copy-start(s32[1,8]{1,0:T(1,128)} %targets.3) | copy-start | bytes 100
  17.4 19.1 %copy-start.1 = (f32[16,16,128]{2,1,0:T(8,128)S(1)}, f32[16,16,128]{2,1,0:T(8,128)}, u32[]{:S(2)}) copy-start(f32[16,16,128]{2,1,0:T(8,128)} %all_to_all.10.gathered) | copy-start | bytes 393220
  27.2 5.7 %copy-start = (bf16[8,1024,1024]{2,1,0:T(8,128)(2,1)}, bf16[8,1024,1024]{2,1,0:T(8,128)(2,1)S(1)}, u32[]{:S(2)}) copy-start(bf16[8,1024,1024]{2,1,0:T(8,128)(2,1)S(1)} %get-tuple-element.10.tiles) | copy-start | bytes 50331652
  32.9 11.5 %all-to-all-start.1 = ((f32[16,40,128]{2,1,0:T(8,128)}), f32[16,40,128]{2,1,0:T(8,128)S(1)}, u32[]{:S(2)}, u32[]{:S(2)}) async-start(f32[16,40,128]{2,1,0:T(8,128)} %get-tuple-element.7), calls=%async_computation.1 | async-start | bytes 655360 | tf_op jit(solution)/shard_map/all_to_all | solution.py:264
  36.5 12.3 %collective-permute-start.3 = (f32[16,16,128]{2,1,0:T(8,128)S(1)}, f32[16,16,128]{2,1,0:T(8,128)S(1)}, u32[]{:S(2)}, u32[]{:S(2)}) collective-permute-start(f32[16,16,128]{2,1,0:T(8,128)S(1)} %copy-done.1), channel_id=1, source_target_pairs={{1,0},{2,1},{3,2},{4,3},{5,4},{6,5},{7,6},{0,7},{9,8},{10,9},{11,1... | collective-permute-start | bytes 393224 | tf_op jit(solution)/shard_map/ppermute | solution.py:251
  38.5 10.2 %collective-permute-start.2 = (f32[16,16,128]{2,1,0:T(8,128)S(1)}, f32[16,16,128]{2,1,0:T(8,128)S(1)}, u32[]{:S(2)}, u32[]{:S(2)}) collective-permute-start(f32[16,16,128]{2,1,0:T(8,128)S(1)} %copy-done.1), channel_id=1, source_target_pairs={{0,1},{1,2},{2,3},{3,4},{4,5},{5,6},{6,7},{7,0},{8,9},{9,10},{10,1... | collective-permute-start | bytes 393224 | tf_op jit(solution)/shard_map/ppermute | solution.py:251
  44.4 13.2 %copy-start.3 = (f32[40,128]{1,0:T(8,128)}, f32[40,128]{1,0:T(8,128)S(1)}, u32[]{:S(2)}) copy-start(f32[40,128]{1,0:T(8,128)S(1)} %reduce_sum.9.sums) | copy-start | bytes 61444
  44.4 13.1 %collective-permute-start.1 = (f32[40,128]{1,0:T(8,128)S(1)}, f32[40,128]{1,0:T(8,128)S(1)}, u32[]{:S(2)}, u32[]{:S(2)}) collective-permute-start(f32[40,128]{1,0:T(8,128)S(1)} %reduce_sum.9.sums), channel_id=1, source_target_pairs={{1,0},{2,1},{3,2},{4,3},{5,4},{6,5},{7,6},{0,7},{9,8},{10,9},{11,1... | collective-permute-start | bytes 61448 | tf_op jit(solution)/shard_map/ppermute | solution.py:251
  47.6 10.0 %collective-permute-start = (f32[40,128]{1,0:T(8,128)S(1)}, f32[40,128]{1,0:T(8,128)S(1)}, u32[]{:S(2)}, u32[]{:S(2)}) collective-permute-start(f32[40,128]{1,0:T(8,128)S(1)} %reduce_sum.9.sums), channel_id=1, source_target_pairs={{0,1},{1,2},{2,3},{3,4},{4,5},{5,6},{6,7},{7,0},{8,9},{9,10},{10,1... | collective-permute-start | bytes 61448 | tf_op jit(solution)/shard_map/ppermute | solution.py:251
  57.6 0.6 %copy-start.4 = (f32[40,128]{1,0:T(8,128)}, f32[40,128]{1,0:T(8,128)S(1)}, u32[]{:S(2)}) copy-start(f32[40,128]{1,0:T(8,128)S(1)} %collective-permute-done.1.east) | copy-start | bytes 61444
  58.2 0.6 copy-start.5

commit v2 on v1

v2 whole, which is shorter than its diff:
```python
import functools

import jax
import jax.numpy as jnp
from jax import lax
from jax.experimental import pallas as pl
from jax.experimental.pallas import tpu as pltpu
from jax.sharding import PartitionSpec as P

RADIX = 128.0
ROWS, COLS = 8, 128
SUM_ROWS = 48
SCOPED = 24 * 2**20
SMALL = 8 * 2**20
CHUNK = 2 * COLS
VMEM_SPEC = pl.BlockSpec(memory_space=pltpu.VMEM)
HBM_SPEC = pl.BlockSpec(memory_space=pltpu.HBM)
SMEM_SPEC = pl.BlockSpec(memory_space=pltpu.SMEM)


def pack_kernel(levels_ref, potential_ref, out_ref):
    packed = levels_ref[0].astype(jnp.float32) * RADIX + levels_ref[1].astype(jnp.float32)
    potential = potential_ref[...]
    for target in range(out_ref.shape[0]):
        out_ref[target, 0:ROWS, :] = packed
        out_ref[target, ROWS : 2 * ROWS, :] = potential


def pack(line_levels, potential, n_lat):
    return pl.pallas_call(
        pack_kernel,
        out_shape=pltpu.VMEM((n_lat, 2 * ROWS, COLS), jnp.float32),
        in_specs=[VMEM_SPEC] * 2,
        out_specs=VMEM_SPEC,
        name="pack_levels_potential",
    )(line_levels, potential)


def row_above(block, edge):
    rows = lax.broadcasted_iota(jnp.int32, block.shape, 0)
    return jnp.where(rows == ROWS - 1, edge, pltpu.roll(block, ROWS - 1, 0))


def row_below(block, edge):
    rows = lax.broadcasted_iota(jnp.int32, block.shape, 0)
    return jnp.where(rows == 0, edge, pltpu.roll(block, 1, 0))


def in_vmem(array):
    return pltpu.with_memory_space_constraint(array, pltpu.VMEM)


def in_hbm(array):
    return pltpu.with_memory_space_constraint(array, pltpu.HBM)


def product_kernel(
    conductivity_hbm, wind_hbm, tiles_hbm, near_plain, near_wind, far_plain_hbm, far_wind_hbm,
    fields, conductivity, wind, tiles, far_plain, far_wind, sems, far_sems,
):
    tile_count, mag_cells, geo_cells = tiles.shape
    levels_n = conductivity.shape[1]
    near_count = near_plain.shape[0]
    order = list(range(near_count, tile_count)) + list(range(near_count))
    field_copies = [
        pltpu.make_async_copy(conductivity_hbm, conductivity, sems.at[tile_count]),
        pltpu.make_async_copy(wind_hbm, wind, sems.at[tile_count + 1]),
    ]
    tile_copies = {
        k: pltpu.make_async_copy(tiles_hbm.at[k], tiles.at[k], sems.at[k]) for k in order
    }
    for copy in field_copies + list(tile_copies.values()):
        copy.start()
    for copy in field_copies:
        copy.wait()
    fields[0:levels_n, :] = conductivity[0]
    fields[levels_n : 2 * levels_n, :] = conductivity[1]
    first, second, third, fourth = (wind[i].astype(jnp.float32) for i in range(4))
    fields[2 * levels_n : 3 * levels_n, :] = (third - second).astype(jnp.bfloat16)
    fields[3 * levels_n : 4 * levels_n, :] = (first + fourth).astype(jnp.bfloat16)
    far_copies = []
    for k in order:
        tile_copies[k].wait()
        near, i = k < near_count, k if k < near_count else k - near_count
        plain_out, wind_out = (near_plain, near_wind) if near else (far_plain, far_wind)
        for start in range(0, mag_cells, CHUNK):
            columns = slice(start, start + CHUNK)
            value = lax.dot_general(
                fields[...],
                tiles[k, columns, :],
                (((1,), (1,)), ((), ())),
                preferred_element_type=jnp.float32,
            )
            plain_out[i, :, columns] = value[: 2 * levels_n].astype(jnp.bfloat16)
            wind_out[i, :, columns] = value[2 * levels_n :]
        if not near:
            copies = [
                pltpu.make_async_copy(far_plain.at[i], far_plain_hbm.at[i], far_sems.at[2 * i]),
                pltpu.make_async_copy(far_wind.at[i], far_wind_hbm.at[i], far_sems.at[2 * i + 1]),
            ]
            for copy in copies:
                copy.start()
            far_copies += copies
    for copy in far_copies:
        copy.wait()


def product(conductivity, wind, tiles, near_count):
    levels_n, geo_cells = conductivity.shape[1:]
    tile_count, mag_cells = tiles.shape[:2]
    far_count = tile_count - near_count
    near_shape, far_shape = ((count, 2 * levels_n, mag_cells) for count in (near_count, far_count))
    return pl.pallas_call(
        product_kernel,
        out_shape=(
            pltpu.VMEM(near_shape, jnp.bfloat16),
            pltpu.VMEM(near_shape, jnp.float32),
            pltpu.HBM(far_shape, jnp.bfloat16),
            pltpu.HBM(far_shape, jnp.float32),
        ),
        in_specs=[HBM_SPEC] * 3,
        out_specs=(VMEM_SPEC, VMEM_SPEC, HBM_SPEC, HBM_SPEC),
        scratch_shapes=[
            pltpu.VMEM((4 * levels_n, geo_cells), jnp.bfloat16),
            pltpu.VMEM(conductivity.shape, conductivity.dtype),
            pltpu.VMEM(wind.shape, wind.dtype),
            pltpu.VMEM(tiles.shape, tiles.dtype),
            pltpu.VMEM(far_shape, jnp.bfloat16),
            pltpu.VMEM(far_shape, jnp.float32),
            pltpu.SemaphoreType.DMA((tile_count + 2,)),
            pltpu.SemaphoreType.DMA((2 * far_count,)),
        ],
        compiler_params=pltpu.CompilerParams(vmem_limit_bytes=SCOPED),
        cost_estimate=pl.CostEstimate(
            flops=2 * 4 * levels_n * tiles.size, bytes_accessed=2 * tiles.size, transcendentals=0
        ),
        name="regrid_product",
    )(conductivity, wind, tiles)


def integral_kernel(
    targets, level_weights, gathered, near_plain, near_wind, far_plain_hbm, far_wind_hbm, combined, edges,
    weights, plain, mirrored, far_plain, far_wind, sems,
):
    near_count, far_count = near_plain.shape[0], far_plain.shape[0]
    levels_n = level_weights.shape[0]
    n_lat = gathered.shape[0]
    copies = [
        (
            pltpu.make_async_copy(far_plain_hbm.at[i], far_plain.at[i], sems.at[2 * i]),
            pltpu.make_async_copy(far_wind_hbm.at[i], far_wind.at[i], sems.at[2 * i + 1]),
        )
        for i in range(far_count)
    ]
    for pair in copies:
        for copy in pair:
            copy.start()
    for level in range(levels_n):
        weights[level : level + 1, :] = jnp.full((1, COLS), level_weights[level], jnp.float32)
    plain[...] = jnp.zeros_like(plain)
    mirrored[...] = jnp.zeros_like(mirrored)
    level_of = lax.broadcasted_iota(jnp.int32, (levels_n, COLS), 0).astype(jnp.float32)
    for k in range(near_count + far_count):
        if k >= near_count:
            for copy in copies[k - near_count]:
                copy.wait()
        near, i = k < near_count, k if k < near_count else k - near_count
        planes = (near_plain, near_wind) if near else (far_plain, far_wind)
        target = targets[0, k]
        for row in range(ROWS):
            bounds = gathered[target, row : row + 1, :]
            low = jnp.floor(bounds * (1.0 / RADIX))
            high = bounds - low * RADIX
            inside = (level_of >= low) & (level_of < high)
            weight = jnp.where(inside, weights[...], 0.0)
            for f in range(4):
                rows = slice(f % 2 * levels_n, (f % 2 + 1) * levels_n)
                part = planes[f // 2][i, rows, row * COLS : (row + 1) * COLS]
                total = jnp.sum(part.astype(jnp.float32) * weight, axis=0, keepdims=True)
                plain[target, f, row : row + 1, :] = total
                mirrored[n_lat - 1 - target, f, ROWS - 1 - row : ROWS - row, :] = total

    lanes = lax.broadcasted_iota(jnp.int32, (ROWS, COLS), 1)
    for f in range(4):
        for b in range(n_lat):
            combined[b, f] = plain[b, f] + mirrored[b, f]

    def both_edges(block_of):
        edge = jnp.zeros((ROWS, COLS), jnp.float32)
        for b in range(n_lat):
            block = block_of(b)
            edge = jnp.where(lanes == 2 * b, pltpu.roll(block, 2 * b, 1), edge)
            edge = jnp.where(lanes == 2 * b + 1, pltpu.roll(block, 2 * b + 2, 1), edge)
        return edge

    for f in range(3):
        edges[f * ROWS : (f + 1) * ROWS, :] = both_edges(lambda b: combined[b, f])
    edges[3 * ROWS : 4 * ROWS, :] = both_edges(lambda b: gathered[b, ROWS : 2 * ROWS, :])


def integral(targets, level_weights, gathered, near, far):
    far_shape = far[0].shape
    n_lat = gathered.shape[0]
    return pl.pallas_call(
        integral_kernel,
        out_shape=(
            pltpu.VMEM((n_lat, 4, ROWS, COLS), jnp.float32),
            pltpu.VMEM((4 * ROWS, COLS), jnp.float32),
        ),
        in_specs=[SMEM_SPEC] * 2 + [VMEM_SPEC] * 3 + [HBM_SPEC] * 2,
        out_specs=(VMEM_SPEC, VMEM_SPEC),
        scratch_shapes=[
            pltpu.VMEM((level_weights.shape[0], COLS), jnp.float32),
            pltpu.VMEM((n_lat, 4, ROWS, COLS), jnp.float32),
            pltpu.VMEM((n_lat, 4, ROWS, COLS), jnp.float32),
            pltpu.VMEM(far_shape, jnp.bfloat16),
            pltpu.VMEM(far_shape, jnp.float32),
            pltpu.SemaphoreType.DMA((2 * far_shape[0],)),
        ],
        compiler_params=pltpu.CompilerParams(vmem_limit_bytes=SCOPED),
        cost_estimate=pl.CostEstimate(
            flops=6 * near[0].size, bytes_accessed=16 * near[0].size, transcendentals=0
        ),
        name="level_integral",
    )(targets, level_weights, in_vmem(gathered), *map(in_vmem, near), *map(in_hbm, far))


def assemble_kernel(combined, west, east, out_ref):
    n_lat = combined.shape[0]
    lanes = lax.broadcasted_iota(jnp.int32, (ROWS, COLS), 1)
    beyond = [
        jnp.where(lanes % 2 == 0, east[f * ROWS : (f + 1) * ROWS, :], west[f * ROWS : (f + 1) * ROWS, :])
        for f in range(3)
    ]
    corners = [pltpu.roll(beyond[1], (COLS - 2 * b) % COLS, 1) for b in range(n_lat)]
    nothing = jnp.zeros((1, COLS), jnp.float32)
    for b in range(n_lat):
        def below(blocks):
            return blocks(b - 1)[ROWS - 1 : ROWS] if b > 0 else nothing

        def above(blocks):
            return blocks(b + 1)[0:1] if b + 1 < n_lat else nothing

        merid = combined[b, 3]
        for f in range(3):
            out_ref[b, f * ROWS : (f + 1) * ROWS, :] = combined[b, f]
        out_ref[b, 24:32, :] = row_below(merid, below(lambda i: combined[i, 3])) - row_above(
            merid, above(lambda i: combined[i, 3])
        )
        out_ref[b, 32:33, :] = below(lambda i: combined[i, 0])
        out_ref[b, 33:34, :] = above(lambda i: combined[i, 0])
        out_ref[b, 34:35, :] = below(lambda i: combined[i, 1])
        out_ref[b, 35:36, :] = above(lambda i: combined[i, 1])
        out_ref[b, 36:37, :] = below(lambda i: corners[i])
        out_ref[b, 37:38, :] = above(lambda i: corners[i])
        out_ref[b, 38:40, :] = jnp.zeros((2, COLS), jnp.float32)
        columns = jnp.zeros((ROWS, COLS), jnp.float32)
        for f in range(3):
            moved = pltpu.roll(beyond[f], (COLS + 2 * f - 2 * b) % COLS, 1)
            columns = jnp.where((lanes >= 2 * f) & (lanes < 2 * f + 2), moved, columns)
        out_ref[b, 40:48, :] = columns


def assemble(combined, west, east):
    return pl.pallas_call(
        assemble_kernel,
        out_shape=jax.ShapeDtypeStruct((combined.shape[0], SUM_ROWS, COLS), jnp.float32),
        in_specs=[VMEM_SPEC] * 3,
        out_specs=VMEM_SPEC,
        compiler_params=pltpu.CompilerParams(vmem_limit_bytes=SMALL),
        name="assemble_sends",
    )(in_vmem(combined), in_vmem(west), in_vmem(east))


def backward_kernel(targets, gathered, west, east, tiles_hbm, out_ref, zonal, merid, rows_ref, tiles, sems):
    n_lat = gathered.shape[0]
    tile_count = tiles.shape[0]
    copies = [
        pltpu.make_async_copy(tiles_hbm.at[k], tiles.at[k], sems.at[k]) for k in range(tile_count)
    ]
    for copy in copies:
        copy.start()
    lanes = lax.broadcasted_iota(jnp.int32, (ROWS, COLS), 1)
    nothing = jnp.zeros((1, COLS), jnp.float32)
    west_edges, east_edges = west[3 * ROWS : 4 * ROWS, :], east[3 * ROWS : 4 * ROWS, :]
    for b in range(n_lat):
        here = gathered[b, ROWS : 2 * ROWS, :]
        shift = COLS - 1 - 2 * b
        eastern = jnp.where(
            lanes == COLS - 1, pltpu.roll(east_edges, shift, 1), pltpu.roll(here, COLS - 1, 1)
        )
        western = jnp.where(lanes == 0, pltpu.roll(west_edges, shift, 1), pltpu.roll(here, 1, 1))
        above = gathered[b + 1, ROWS : ROWS + 1, :] if b + 1 < n_lat else nothing
        below = gathered[b - 1, 2 * ROWS - 1 : 2 * ROWS, :] if b > 0 else nothing
        zonal[b] = -0.5 * (eastern - western)
        merid[b] = -0.5 * (row_above(here, above) - row_below(here, below))
    rows_ref[...] = jnp.zeros_like(rows_ref)
    for k in range(tile_count):
        target = targets[0, k]
        for row in range(ROWS):
            columns = slice(row * COLS, (row + 1) * COLS)
            rows_ref[k, 0:1, columns] = zonal[target, row : row + 1, :]
            rows_ref[k, 1:2, columns] = merid[target, row : row + 1, :]
    total = jnp.zeros((ROWS, tiles.shape[2]), jnp.float32)
    for k in range(tile_count):
        copies[k].wait()
        total += jnp.dot(
            rows_ref[k].astype(jnp.bfloat16), tiles[k], preferred_element_type=jnp.float32
        )
    out_ref[...] = total[0:2]


def backward(targets, gathered, west, east, tiles):
    n_lat = gathered.shape[0]
    tile_count, mag_cells, geo_cells = tiles.shape
    return pl.pallas_call(
        backward_kernel,
        out_shape=jax.ShapeDtypeStruct((2, geo_cells), jnp.float32),
        in_specs=[SMEM_SPEC, VMEM_SPEC, VMEM_SPEC, VMEM_SPEC, HBM_SPEC],
        out_specs=VMEM_SPEC,
        scratch_shapes=[
            pltpu.VMEM((n_lat, ROWS, COLS), jnp.float32),
            pltpu.VMEM((n_lat, ROWS, COLS), jnp.float32),
            pltpu.VMEM((tile_count, ROWS, mag_cells), jnp.float32),
            pltpu.VMEM(tiles.shape, tiles.dtype),
            pltpu.SemaphoreType.DMA((tile_count,)),
        ],
        compiler_params=pltpu.CompilerParams(vmem_limit_bytes=SCOPED),
        cost_estimate=pl.CostEstimate(
            flops=16 * tiles.size, bytes_accessed=2 * tiles.size, transcendentals=0
        ),
        name="electric_to_geo",
    )(targets, in_vmem(gathered), in_vmem(west), in_vmem(east), tiles)


def stencil_kernel(received, stencil_ref, source_ref):
    sums = received[0]
    for source in range(1, received.shape[0]):
        sums += received[source]
    lanes = lax.broadcasted_iota(jnp.int32, (ROWS, COLS), 1)
    columns = sums[40:48]

    def eastward(block, beyond, lane):
        moved = pltpu.roll(beyond, COLS - 1 - lane, 1)
        return jnp.where(lanes == COLS - 1, moved, pltpu.roll(block, COLS - 1, 1))

    def westward(block, beyond, lane):
        moved = pltpu.roll(beyond, (COLS - lane) % COLS, 1)
        return jnp.where(lanes == 0, moved, pltpu.roll(block, 1, 1))

    center0, center1, zonal, merid, edge = (sums[i * ROWS : (i + 1) * ROWS] for i in range(5))
    corner = pltpu.roll(edge, ROWS - 2, 0)
    edge_east, edge_west = eastward(edge, corner, 0), westward(edge, corner, 1)
    east1, west1 = eastward(center1, columns, 2), westward(center1, columns, 3)
    east_coef = 0.5 * (center0 + eastward(center0, columns, 0))
    west_coef = 0.5 * (center0 + westward(center0, columns, 1))
    north_coef = 0.5 * (center0 + row_above(center0, edge[1:2]))
    south_coef = 0.5 * (center0 + row_below(center0, edge[0:1]))
    ne_coef = 0.25 * (row_above(east1, edge_east[3:4]) - center1)
    nw_coef = -0.25 * (row_above(west1, edge_west[3:4]) - center1)
    se_coef = -0.25 * (row_below(east1, edge_east[2:3]) - center1)
    sw_coef = 0.25 * (row_below(west1, edge_west[2:3]) - center1)
    others = [east_coef, west_coef, north_coef, south_coef, ne_coef, nw_coef, se_coef, sw_coef]
    stencil_ref[0] = -sum(others[1:], others[0])
    for i, coef in enumerate(others):
        stencil_ref[i + 1] = coef
    source_ref[...] = (
        0.5 * (eastward(zonal, columns, 4) - westward(zonal, columns, 5)) + 0.5 * merid
    )


def stencil_source(received):
    return pl.pallas_call(
        stencil_kernel,
        out_shape=(
            jax.ShapeDtypeStruct((9, ROWS, COLS), jnp.float32),
            jax.ShapeDtypeStruct((ROWS, COLS), jnp.float32),
        ),
        in_specs=[VMEM_SPEC],
        out_specs=(VMEM_SPEC, VMEM_SPEC),
        compiler_params=pltpu.CompilerParams(vmem_limit_bytes=SMALL),
        name="stencil_source",
    )(in_vmem(received))


def lon_neighbours(block):
    count = lax.axis_size("lon")
    from_west = [(i, (i + 1) % count) for i in range(count)]
    from_east = [((i + 1) % count, i) for i in range(count)]
    return lax.ppermute(block, "lon", from_west), lax.ppermute(block, "lon", from_east)


def per_device(
    conductivity, wind_terms, correlation_tiles, tile_targets, level_weights, line_levels, potential
):
    n_lat = lax.axis_size("lat")
    tiles = in_hbm(correlation_tiles)
    near_count = tiles.shape[0] // 2
    packed = pack(line_levels, potential, n_lat)
    gathered = lax.all_to_all(packed, "lat", 0, 0, tiled=True)
    near_plain, near_wind, far_plain, far_wind = product(in_hbm(conductivity), in_hbm(wind_terms), tiles, near_count)
    combined, edges = integral(tile_targets, level_weights, gathered, (near_plain, near_wind), (far_plain, far_wind))
    west, east = lon_neighbours(edges)
    sends = assemble(combined, west, east)
    received = lax.all_to_all(sends, "lat", 0, 0, tiled=True)
    geo_field = backward(tile_targets, gathered, west, east, tiles)
    stencil, source_term = stencil_source(received)
    return stencil, source_term, geo_field


def solution(mesh):
    in_specs = (
        P(None, None, ("lat", "lon")),
        P(None, None, ("lat", "lon")),
        P(("lat", "lon"), None, None),
        P(("lat", "lon"), None),
        P(),
        P(None, "lat", "lon"),
        P("lat", "lon"),
    )
    out_specs = (P(None, "lat", "lon"), P("lat", "lon"), P(None, ("lat", "lon")))
    return jax.shard_map(
        per_device, mesh=mesh, in_specs=in_specs, out_specs=out_specs, check_vma=False
    )
```

time: 60.7 us -> 46 us (0.76)
  the two profiles are of different devices: /device:TPU:1 before, /device:TPU:0 now
where the time goes in v2:
time: 46 us; the launch traced here: 45.6 us
  Pallas kernels  21.6 us (47%)
  starting transfers between devices  17.1 us (37%)
  waiting for transfers between devices  6.25 us (14%)
  between operations  0.71 us (2%)
    pallas_call x1, Pallas kernels, product(): pl.pallas_call(product_kernel, out_shape=(pltpu.VMEM(near_shape, jnp.bflo...  8.3 us
    all_to_all x1, starting transfers between devices, per_device(): gathered = lax.all_to_all(packed, 'lat', 0, 0, tiled=True)  7.96 us
    pallas_call x1, Pallas kernels, backward(): pl.pallas_call(backward_kernel, out_shape=jax.ShapeDtypeStruct((2, geo_ce...  7.51 us
    all_to_all x1, starting transfers between devices, per_device(): received = lax.all_to_all(sends, 'lat', 0, 0, tiled=True)  6.93 us
    ppermute x1, waiting for transfers between devices, lon_neighbours(): lax.ppermute(block, 'lon', from_west)  2.93 us
    pallas_call x1, Pallas kernels, integral(): pl.pallas_call(integral_kernel, out_shape=(pltpu.VMEM((n_lat, 4, ROWS, CO...  2.81 us
    ppermute x1, starting transfers between devices, lon_neighbours(): lax.ppermute(block, 'lon', from_east)  2.18 us
    all_to_all x1, waiting for transfers between devices, per_device(): received = lax.all_to_all(sends, 'lat', 0, 0, tiled=True)  1.87 us
  transfers between devices with their start and end apart: 4, of which 3 were waited for; matrix products, arithmetic and copies ran while one was open for 0% of the time, Pallas kernels for 35%

profile of v2, /device:TPU:0, one launch (start us, length us, event | category | flops | bytes accessed | tf_op | source)
XLA Modules:
  0.0 45.6 jit_solution(4945626782065895917)
XLA Ops:
  0.6 1.4 %pack_levels_potential.1 = f32[16,16,128]{2,1,0:T(8,128)} custom-call(s32[2,8,128]{2,1,0:T(8,128)} %levels_ref.1, f32[8,128]{1,0:T(8,128)} %potential_ref.1), custom_call_target="tpu_custom_call" | custom-call | tf_op jit(solution)/shard_map/pack_levels_potential/pallas_call | solution.py:30
  2.0 8.0 %all-to-all-start = ((f32[16,16,128]{2,1,0:T(8,128)}), f32[16,16,128]{2,1,0:T(8,128)S(1)}, u32[]{:S(2)}, u32[]{:S(2)}) async-start(f32[16,16,128]{2,1,0:T(8,128)} %pack_levels_potential.1), calls=%async_computation | async-start | bytes 262144 | tf_op jit(solution)/shard_map/all_to_all | solution.py:400
  10.0 0.0 copy-start
  10.0 0.0 copy-start.1
  10.0 8.3 %regrid_product.1 = (bf16[4,128,1024]{2,1,0:T(8,128)(2,1)S(1)}, f32[4,128,1024]{2,1,0:T(8,128)S(1)}, bf16[4,128,1024]{2,1,0:T(8,128)(2,1)}, f32[4,128,1024]{2,1,0:T(8,128)}) custom-call(bf16[2,64,1024]{2,1,0:T(8,128)(2,1)} %conductivity_hbm.1, bf16[4,64,1024]{2,1,0:T(8,128)(2,1)} %wind_hbm.1, bf16[8,1024,1024]{2,1,0:T(8,128)(2,1)} %tiles_hbm.3), custom_call_target="tpu_custom_call" | custom-call | flops 4294967296 | bytes 16777216 | tf_op jit(solution)/shard_map/regrid_product/pallas_call | solution.py:113
  18.3 0.0 all-to-all-done.gathered
  18.3 0.0 copy-done
  18.3 0.0 copy-done.1
  18.3 2.8 %level_integral.1 = (f32[16,4,8,128]{3,2,1,0:T(8,128)S(1)}, f32[32,128]{1,0:T(8,128)S(1)}) custom-call(s32[1,8]{1,0:T(1,128)S(1)} %copy-done, f32[64]{0:T(128)S(1)} %copy-done.1, f32[16,16,128]{2,1,0:T(8,128)S(1)} %all-to-all-done.gathered, bf16[4,128,1024]{2,1,0:T(8,128)(2,1)S(1)} %get-tuple-element.11.near_plain, ...), custom_call_target="tpu_custom_call" | custom-call | flops 3145728 | bytes 8388608 | tf_op jit(solution)/shard_map/level_integral/pallas_call | solution.py:204
  21.1 2.2 %collective-permute-start.1 = (f32[32,128]{1,0:T(8,128)S(1)}, f32[32,128]{1,0:T(8,128)S(1)}, u32[]{:S(2)}, u32[]{:S(2)}) collective-permute-start(f32[32,128]{1,0:T(8,128)S(1)} %get-tuple-element.16), channel_id=1, source_target_pairs={{1,0},{2,1},{3,2},{4,3},{5,4},{6,5},{7,6},{0,7},{9,8},{10,9},{11,1... | collective-permute-start | bytes 49160 | tf_op jit(solution)/shard_map/ppermute | solution.py:390
  23.3 0.0 collective-permute-start
  23.3 1.4 %collective-permute-done.1.east = f32[32,128]{1,0:T(8,128)S(1)} collective-permute-done((f32[32,128]{1,0:T(8,128)S(1)}, f32[32,128]{1,0:T(8,128)S(1)}, u32[]{:S(2)}, u32[]{:S(2)}) %collective-permute-start.1) | collective-permute-done | bytes 16416 | tf_op jit(solution)/shard_map/ppermute | solution.py:390
  24.8 2.9 %collective-permute-done.west = f32[32,128]{1,0:T(8,128)S(1)} collective-permute-done((f32[32,128]{1,0:T(8,128)S(1)}, f32[32,128]{1,0:T(8,128)S(1)}, u32[]{:S(2)}, u32[]{:S(2)}) %collective-permute-start) | collective-permute-done | bytes 16416 | tf_op jit(solution)/shard_map/ppermute | solution.py:390
  27.7 0.9 %assemble_sends.1 = f32[16,48,128]{2,1,0:T(8,128)} custom-call(f32[16,4,8,128]{3,2,1,0:T(8,128)S(1)} %get-tuple-element.15.combined, f32[32,128]{1,0:T(8,128)S(1)} %collective-permute-done.west, f32[32,128]{1,0:T(8,128)S(1)} %collective-permute-done.1.east), custom_call_target="tpu_custom_call" | custom-call | tf_op jit(solution)/shard_map/assemble_sends/pallas_call | solution.py:265
  28.6 6.9 %all-to-all-start.1 = ((f32[16,48,128]{2,1,0:T(8,128)}), f32[16,48,128]{2,1,0:T(8,128)S(1)}, u32[]{:S(2)}, u32[]{:S(2)}) async-start(f32[16,48,128]{2,1,0:T(8,128)} %assemble_sends.1), calls=%async_computation.1 | async-start | bytes 786432 | tf_op jit(solution)/shard_map/all_to_all | solution.py:405
  35.5 7.5 %electric_to_geo.1 = f32[2,1024]{1,0:T(2,128)} custom-call(s32[1,8]{1,0:T(1,128)S(1)} %copy-done, f32[16,16,128]{2,1,0:T(8,128)S(1)} %all-to-all-done.gathered, f32[32,128]{1,0:T(8,128)S(1)} %collective-permute-done.west, f32[32,128]{1,0:T(8,128)S(1)} %collective-permute-done.1.east, bf16[8,1024,1024]{2,1,0:T(8,128)(2,1)} %tiles_hbm.3), custom_call_target="tpu_custom_call" | custom-call | flops 134217728 | bytes 16777216 | tf_op jit(solution)/shard_map/electric_to_geo/pallas_call | solution.py:316
  43.0 1.9 %all-to-all-done.1.received = f32[16,48,128]{2,1,0:T(8,128)S(1)} async-done(((f32[16,48,128]{2,1,0:T(8,128)}), f32[16,48,128]{2,1,0:T(8,128)S(1)}, u32[]{:S(2)}, u32[]{:S(2)}) %all-to-all-start.1) | async-done | bytes 393248 | tf_op jit(solution)/shard_map/all_to_all | solution.py:405
  44.9 0.7 %stencil_source.1 = (f32[9,8,128]{2,1,0:T(8,128)}, f32[8,128]{1,0:T(8,128)}) custom-call(f32[16,48,128]{2,1,0:T(8,128)S(1)} %all-to-all-done.1.received), custom_call_target="tpu_custom_call" | custom-call | tf_op jit(solution)/shard_map/stencil_source/pallas_call | solution.py:373
Async XLA Ops:
  2.0 16.3 %all-to-all-start = ((f32[16,16,128]{2,1,0:T(8,128)}), f32[16,16,128]{2,1,0:T(8,128)S(1)}, u32[]{:S(2)}, u32[]{:S(2)}) async-start(f32[16,16,128]{2,1,0:T(8,128)} %pack_levels_potential.1), calls=%async_computation | async-start | bytes 262144 | tf_op jit(solution)/shard_map/all_to_all | solution.py:400
  10.0 8.3 %copy-start = (s32[1,8]{1,0:T(1,128)S(1)}, s32[1,8]{1,0:T(1,128)}, u32[]{:S(2)}) copy-start(s32[1,8]{1,0:T(1,128)} %targets.3) | copy-start | bytes 100
  10.0 8.3 %copy-start.1 = (f32[64]{0:T(128)S(1)}, f32[64]{0:T(128)}, u32[]{:S(2)}) copy-start(f32[64]{0:T(128)} %level_weights.1) | copy-start | bytes 772
  21.1 3.6 %collective-permute-start.1 = (f32[32,128]{1,0:T(8,128)S(1)}, f32[32,128]{1,0:T(8,128)S(1)}, u32[]{:S(2)}, u32[]{:S(2)}) collective-permute-start(f32[32,128]{1,0:T(8,128)S(1)} %get-tuple-element.16), channel_id=1, source_target_pairs={{1,0},{2,1},{3,2},{4,3},{5,4},{6,5},{7,6},{0,7},{9,8},{10,9},{11,1... | collective-permute-start | bytes 49160 | tf_op jit(solution)/shard_map/ppermute | solution.py:390
  23.3 4.4 %collective-permute-start = (f32[32,128]{1,0:T(8,128)S(1)}, f32[32,128]{1,0:T(8,128)S(1)}, u32[]{:S(2)}, u32[]{:S(2)}) collective-permute-start(f32[32,128]{1,0:T(8,128)S(1)} %get-tuple-element.16), channel_id=1, source_target_pairs={{0,1},{1,2},{2,3},{3,4},{4,5},{5,6},{6,7},{7,0},{8,9},{9,10},{10,1... | collective-permute-start | bytes 49160 | tf_op jit(solution)/shard_map/ppermute | solution.py:390
  28.6 16.3 %all-to-all-start.1 = ((f32[16,48,128]{2,1,0:T(8,128)}), f32[16,48,128]{2,1,0:T(8,128)S(1)}, u32[]{:S(2)}, u32[]{:S(2)}) async-start(f32[16,48,128]{2,1,0:T(8,128)} %assemble_sends.1), calls=%async_computation.1 | async-start | bytes 786432 | tf_op jit(solution)/shard_map/all_to_all | solution.py:405

commit v3 on v2

--- a/solution.py
+++ b/solution.py
@@ -225,13 +225,14 @@
     )(targets, level_weights, in_vmem(gathered), *map(in_vmem, near), *map(in_hbm, far))
 
 
-def assemble_kernel(combined, west, east, out_ref):
+def assemble_kernel(combined, inside, across, out_ref):
     n_lat = combined.shape[0]
     lanes = lax.broadcasted_iota(jnp.int32, (ROWS, COLS), 1)
-    beyond = [
-        jnp.where(lanes % 2 == 0, east[f * ROWS : (f + 1) * ROWS, :], west[f * ROWS : (f + 1) * ROWS, :])
-        for f in range(3)
-    ]
+    beyond = []
+    for f in range(3):
+        rows = slice(f * ROWS, (f + 1) * ROWS)
+        west, east = west_and_east(inside[rows, :], across[rows, :])
+        beyond.append(jnp.where(lanes % 2 == 0, east, west))
     corners = [pltpu.roll(beyond[1], (COLS - 2 * b) % COLS, 1) for b in range(n_lat)]
     nothing = jnp.zeros((1, COLS), jnp.float32)
     for b in range(n_lat):
@@ -261,7 +262,7 @@
         out_ref[b, 40:48, :] = columns
 
 
-def assemble(combined, west, east):
+def assemble(combined, inside, across):
     return pl.pallas_call(
         assemble_kernel,
         out_shape=jax.ShapeDtypeStruct((combined.shape[0], SUM_ROWS, COLS), jnp.float32),
@@ -269,10 +270,10 @@
         out_specs=VMEM_SPEC,
         compiler_params=pltpu.CompilerParams(vmem_limit_bytes=SMALL),
         name="assemble_sends",
-    )(in_vmem(combined), in_vmem(west), in_vmem(east))
-
-
-def backward_kernel(targets, gathered, west, east, tiles_hbm, out_ref, zonal, merid, rows_ref, tiles, sems):
+    )(in_vmem(combined), in_vmem(inside), in_vmem(across))
+
+
+def backward_kernel(targets, gathered, inside, across, tiles_hbm, out_ref, zonal, merid, rows_ref, tiles, sems):
     n_lat = gathered.shape[0]
     tile_count = tiles.shape[0]
     copies = [
@@ -282,7 +283,7 @@
         copy.start()
     lanes = lax.broadcasted_iota(jnp.int32, (ROWS, COLS), 1)
     nothing = jnp.zeros((1, COLS), jnp.float32)
-    west_edges, east_edges = west[3 * ROWS : 4 * ROWS, :], east[3 * ROWS : 4 * ROWS, :]
+    west_edges, east_edges = west_and_east(inside[3 * ROWS :, :], across[3 * ROWS :, :])
     for b in range(n_lat):
         here = gathered[b, ROWS : 2 * ROWS, :]
         shift = COLS - 1 - 2 * b
@@ -310,7 +311,7 @@
     out_ref[...] = total[0:2]
 
 
-def backward(targets, gathered, west, east, tiles):
+def backward(targets, gathered, inside, across, tiles):
     n_lat = gathered.shape[0]
     tile_count, mag_cells, geo_cells = tiles.shape
     return pl.pallas_call(
@@ -330,7 +331,7 @@
             flops=16 * tiles.size, bytes_accessed=2 * tiles.size, transcendentals=0
         ),
         name="electric_to_geo",
-    )(targets, in_vmem(gathered), in_vmem(west), in_vmem(east), tiles)
+    )(targets, in_vmem(gathered), in_vmem(inside), in_vmem(across), tiles)
 
 
 def stencil_kernel(received, stencil_ref, source_ref):
@@ -385,9 +386,14 @@
 
 def lon_neighbours(block):
     count = lax.axis_size("lon")
-    from_west = [(i, (i + 1) % count) for i in range(count)]
-    from_east = [((i + 1) % count, i) for i in range(count)]
-    return lax.ppermute(block, "lon", from_west), lax.ppermute(block, "lon", from_east)
+    inside = [(i, i ^ 1) for i in range(count)]
+    across = [(i, (i + 1 if i % 2 else i - 1) % count) for i in range(count)]
+    return lax.ppermute(block, "lon", inside), lax.ppermute(block, "lon", across)
+
+
+def west_and_east(inside, across):
+    even = lax.axis_index("lon") % 2 == 0
+    return jnp.where(even, across, inside), jnp.where(even, inside, across)
 
 
 def per_device(
@@ -400,10 +406,10 @@
     gathered = lax.all_to_all(packed, "lat", 0, 0, tiled=True)
     near_plain, near_wind, far_plain, far_wind = product(in_hbm(conductivity), in_hbm(wind_terms), tiles, near_count)
     combined, edges = integral(tile_targets, level_weights, gathered, (near_plain, near_wind), (far_plain, far_wind))
-    west, east = lon_neighbours(edges)
-    sends = assemble(combined, west, east)
+    inside, across = lon_neighbours(edges)
+    sends = assemble(combined, inside, across)
     received = lax.all_to_all(sends, "lat", 0, 0, tiled=True)
-    geo_field = backward(tile_targets, gathered, west, east, tiles)
+    geo_field = backward(tile_targets, gathered, inside, across, tiles)
     stencil, source_term = stencil_source(received)
     return stencil, source_term, geo_field
 

time: 46 us -> 44.2 us (0.961)
  waiting for transfers between devices: 6.25 us -> 4.06 us
    ppermute x2, waiting for transfers between devices: 4.37 us -> 2.2 us  [the longest x1 2.2 us: lon_neighbours(): lax.ppermute(block, 'lon', across)]
  transfers between devices with their start and end apart: 4 -> 4, of which waited for: 3 -> 2; matrix products, arithmetic and copies ran while one was open for 0% -> 0% of each run, Pallas kernels for 35% -> 36%
where the time goes in v3:
time: 44.2 us; the launch traced here: 43.8 us
  Pallas kernels  21.6 us (49%)
  starting transfers between devices  17.4 us (39%)
  waiting for transfers between devices  4.06 us (9%)
  between operations  0.71 us (2%)
    pallas_call x1, Pallas kernels, product(): pl.pallas_call(product_kernel, out_shape=(pltpu.VMEM(near_shape, jnp.bflo...  8.3 us
    all_to_all x1, starting transfers between devices, per_device(): gathered = lax.all_to_all(packed, 'lat', 0, 0, tiled=True)  7.96 us
    pallas_call x1, Pallas kernels, backward(): pl.pallas_call(backward_kernel, out_shape=jax.ShapeDtypeStruct((2, geo_ce...  7.53 us
    all_to_all x1, starting transfers between devices, per_device(): received = lax.all_to_all(sends, 'lat', 0, 0, tiled=True)  7.21 us
    pallas_call x1, Pallas kernels, integral(): pl.pallas_call(integral_kernel, out_shape=(pltpu.VMEM((n_lat, 4, ROWS, CO...  2.81 us
    ppermute x1, starting transfers between devices, lon_neighbours(): lax.ppermute(block, 'lon', across)  2.25 us
    ppermute x1, waiting for transfers between devices, lon_neighbours(): lax.ppermute(block, 'lon', across)  2.2 us
    all_to_all x1, waiting for transfers between devices, per_device(): received = lax.all_to_all(sends, 'lat', 0, 0, tiled=True)  1.86 us
  transfers between devices with their start and end apart: 4, of which 2 were waited for; matrix products, arithmetic and copies ran while one was open for 0% of the time, Pallas kernels for 36%

profile of v3, /device:TPU:0, one launch (start us, length us, event | category | flops | bytes accessed | tf_op | source)
XLA Modules:
  0.0 43.8 jit_solution(4040158171949169431)
XLA Ops:
  0.6 1.4 %pack_levels_potential.1 = f32[16,16,128]{2,1,0:T(8,128)} custom-call(s32[2,8,128]{2,1,0:T(8,128)} %levels_ref.1, f32[8,128]{1,0:T(8,128)} %potential_ref.1), custom_call_target="tpu_custom_call" | custom-call | tf_op jit(solution)/shard_map/pack_levels_potential/pallas_call | solution.py:30
  2.0 8.0 %all-to-all-start = ((f32[16,16,128]{2,1,0:T(8,128)}), f32[16,16,128]{2,1,0:T(8,128)S(1)}, u32[]{:S(2)}, u32[]{:S(2)}) async-start(f32[16,16,128]{2,1,0:T(8,128)} %pack_levels_potential.1), calls=%async_computation | async-start | bytes 262144 | tf_op jit(solution)/shard_map/all_to_all | solution.py:406
  10.0 0.0 copy-start
  10.0 0.0 copy-start.1
  10.0 8.3 %regrid_product.1 = (bf16[4,128,1024]{2,1,0:T(8,128)(2,1)S(1)}, f32[4,128,1024]{2,1,0:T(8,128)S(1)}, bf16[4,128,1024]{2,1,0:T(8,128)(2,1)}, f32[4,128,1024]{2,1,0:T(8,128)}) custom-call(bf16[2,64,1024]{2,1,0:T(8,128)(2,1)} %conductivity_hbm.1, bf16[4,64,1024]{2,1,0:T(8,128)(2,1)} %wind_hbm.1, bf16[8,1024,1024]{2,1,0:T(8,128)(2,1)} %tiles_hbm.3), custom_call_target="tpu_custom_call" | custom-call | flops 4294967296 | bytes 16777216 | tf_op jit(solution)/shard_map/regrid_product/pallas_call | solution.py:113
  18.3 0.0 all-to-all-done.gathered
  18.3 0.0 copy-done
  18.3 0.0 copy-done.1
  18.3 2.8 %level_integral.1 = (f32[16,4,8,128]{3,2,1,0:T(8,128)S(1)}, f32[32,128]{1,0:T(8,128)S(1)}) custom-call(s32[1,8]{1,0:T(1,128)S(1)} %copy-done, f32[64]{0:T(128)S(1)} %copy-done.1, f32[16,16,128]{2,1,0:T(8,128)S(1)} %all-to-all-done.gathered, bf16[4,128,1024]{2,1,0:T(8,128)(2,1)S(1)} %get-tuple-element.11.near_plain, ...), custom_call_target="tpu_custom_call" | custom-call | flops 3145728 | bytes 8388608 | tf_op jit(solution)/shard_map/level_integral/pallas_call | solution.py:204
  21.1 2.3 %collective-permute-start.1 = (f32[32,128]{1,0:T(8,128)S(1)}, f32[32,128]{1,0:T(8,128)S(1)}, u32[]{:S(2)}, u32[]{:S(2)}) collective-permute-start(f32[32,128]{1,0:T(8,128)S(1)} %get-tuple-element.16), channel_id=1, source_target_pairs={{0,7},{1,2},{2,1},{3,4},{4,3},{5,6},{6,5},{7,0},{8,15},{9,10},{10,... | collective-permute-start | bytes 49160 | tf_op jit(solution)/shard_map/ppermute | solution.py:391
  23.4 0.0 collective-permute-start
  23.4 2.2 %collective-permute-done.1.across = f32[32,128]{1,0:T(8,128)S(1)} collective-permute-done((f32[32,128]{1,0:T(8,128)S(1)}, f32[32,128]{1,0:T(8,128)S(1)}, u32[]{:S(2)}, u32[]{:S(2)}) %collective-permute-start.1) | collective-permute-done | bytes 16416 | tf_op jit(solution)/shard_map/ppermute | solution.py:391
  25.6 0.0 collective-permute-done.inside
  25.6 0.9 %assemble_sends.1 = f32[16,48,128]{2,1,0:T(8,128)} custom-call(f32[16,4,8,128]{3,2,1,0:T(8,128)S(1)} %get-tuple-element.15.combined, f32[32,128]{1,0:T(8,128)S(1)} %collective-permute-done.inside, f32[32,128]{1,0:T(8,128)S(1)} %collective-permute-done.1.across), custom_call_target="tpu_custom_call" | custom-call | tf_op jit(solution)/shard_map/assemble_sends/pallas_call | solution.py:266
  26.5 7.2 %all-to-all-start.1 = ((f32[16,48,128]{2,1,0:T(8,128)}), f32[16,48,128]{2,1,0:T(8,128)S(1)}, u32[]{:S(2)}, u32[]{:S(2)}) async-start(f32[16,48,128]{2,1,0:T(8,128)} %assemble_sends.1), calls=%async_computation.1 | async-start | bytes 786432 | tf_op jit(solution)/shard_map/all_to_all | solution.py:411
  33.7 7.5 %electric_to_geo.1 = f32[2,1024]{1,0:T(2,128)} custom-call(s32[1,8]{1,0:T(1,128)S(1)} %copy-done, f32[16,16,128]{2,1,0:T(8,128)S(1)} %all-to-all-done.gathered, f32[32,128]{1,0:T(8,128)S(1)} %collective-permute-done.inside, f32[32,128]{1,0:T(8,128)S(1)} %collective-permute-done.1.across, bf16[8,1024,1024]{2,1,0:T(8,128)(2,1)} %tiles_hbm.3), custom_call_target="tpu_custom_call" | custom-call | flops 134217728 | bytes 16777216 | tf_op jit(solution)/shard_map/electric_to_geo/pallas_call | solution.py:317
  41.2 1.9 %all-to-all-done.1.received = f32[16,48,128]{2,1,0:T(8,128)S(1)} async-done(((f32[16,48,128]{2,1,0:T(8,128)}), f32[16,48,128]{2,1,0:T(8,128)S(1)}, u32[]{:S(2)}, u32[]{:S(2)}) %all-to-all-start.1) | async-done | bytes 393248 | tf_op jit(solution)/shard_map/all_to_all | solution.py:411
  43.1 0.7 %stencil_source.1 = (f32[9,8,128]{2,1,0:T(8,128)}, f32[8,128]{1,0:T(8,128)}) custom-call(f32[16,48,128]{2,1,0:T(8,128)S(1)} %all-to-all-done.1.received), custom_call_target="tpu_custom_call" | custom-call | tf_op jit(solution)/shard_map/stencil_source/pallas_call | solution.py:374
Async XLA Ops:
  2.0 16.3 %all-to-all-start = ((f32[16,16,128]{2,1,0:T(8,128)}), f32[16,16,128]{2,1,0:T(8,128)S(1)}, u32[]{:S(2)}, u32[]{:S(2)}) async-start(f32[16,16,128]{2,1,0:T(8,128)} %pack_levels_potential.1), calls=%async_computation | async-start | bytes 262144 | tf_op jit(solution)/shard_map/all_to_all | solution.py:406
  10.0 8.3 %copy-start = (s32[1,8]{1,0:T(1,128)S(1)}, s32[1,8]{1,0:T(1,128)}, u32[]{:S(2)}) copy-start(s32[1,8]{1,0:T(1,128)} %targets.3) | copy-start | bytes 100
  10.0 8.3 %copy-start.1 = (f32[64]{0:T(128)S(1)}, f32[64]{0:T(128)}, u32[]{:S(2)}) copy-start(f32[64]{0:T(128)} %level_weights.1) | copy-start | bytes 772
  21.1 4.5 %collective-permute-start.1 = (f32[32,128]{1,0:T(8,128)S(1)}, f32[32,128]{1,0:T(8,128)S(1)}, u32[]{:S(2)}, u32[]{:S(2)}) collective-permute-start(f32[32,128]{1,0:T(8,128)S(1)} %get-tuple-element.16), channel_id=1, source_target_pairs={{0,7},{1,2},{2,1},{3,4},{4,3},{5,6},{6,5},{7,0},{8,15},{9,10},{10,... | collective-permute-start | bytes 49160 | tf_op jit(solution)/shard_map/ppermute | solution.py:391
  23.4 2.2 %collective-permute-start = (f32[32,128]{1,0:T(8,128)S(1)}, f32[32,128]{1,0:T(8,128)S(1)}, u32[]{:S(2)}, u32[]{:S(2)}) collective-permute-start(f32[32,128]{1,0:T(8,128)S(1)} %get-tuple-element.16), channel_id=1, source_target_pairs={{0,1},{1,0},{2,3},{3,2},{4,5},{5,4},{6,7},{7,6},{8,9},{9,8},{10,11... | collective-permute-start | bytes 49160 | tf_op jit(solution)/shard_map/ppermute | solution.py:391
  26.5 16.6 %all-to-all-start.1 = ((f32[16,48,128]{2,1,0:T(8,128)}), f32[16,48,128]{2,1,0:T(8,128)S(1)}, u32[]{:S(2)}, u32[]{:S(2)}) async-start(f32[16,48,128]{2,1,0:T(8,128)} %assemble_sends.1), calls=%async_computation.1 | async-start | bytes 786432 | tf_op jit(solution)/shard_map/all_to_all | solution.py:411

commit v4 on v3

--- a/solution.py
+++ b/solution.py
@@ -9,7 +9,7 @@
 
 RADIX = 128.0
 ROWS, COLS = 8, 128
-SUM_ROWS = 48
+SUM_ROWS = 64
 SCOPED = 24 * 2**20
 SMALL = 8 * 2**20
 CHUNK = 2 * COLS
@@ -66,10 +66,10 @@
         pltpu.make_async_copy(conductivity_hbm, conductivity, sems.at[tile_count]),
         pltpu.make_async_copy(wind_hbm, wind, sems.at[tile_count + 1]),
     ]
-    tile_copies = {
-        k: pltpu.make_async_copy(tiles_hbm.at[k], tiles.at[k], sems.at[k]) for k in order
-    }
-    for copy in field_copies + list(tile_copies.values()):
+    def tile_copy(k):
+        return pltpu.make_async_copy(tiles_hbm.at[k], tiles.at[k], sems.at[k])
+
+    for copy in field_copies + [tile_copy(k) for k in order]:
         copy.start()
     for copy in field_copies:
         copy.wait()
@@ -78,11 +78,8 @@
     first, second, third, fourth = (wind[i].astype(jnp.float32) for i in range(4))
     fields[2 * levels_n : 3 * levels_n, :] = (third - second).astype(jnp.bfloat16)
     fields[3 * levels_n : 4 * levels_n, :] = (first + fourth).astype(jnp.bfloat16)
-    far_copies = []
-    for k in order:
-        tile_copies[k].wait()
-        near, i = k < near_count, k if k < near_count else k - near_count
-        plain_out, wind_out = (near_plain, near_wind) if near else (far_plain, far_wind)
+    def multiply(k, plain_out, wind_out, i):
+        tile_copy(k).wait()
         for start in range(0, mag_cells, CHUNK):
             columns = slice(start, start + CHUNK)
             value = lax.dot_general(
@@ -93,16 +90,26 @@
             )
             plain_out[i, :, columns] = value[: 2 * levels_n].astype(jnp.bfloat16)
             wind_out[i, :, columns] = value[2 * levels_n :]
-        if not near:
-            copies = [
-                pltpu.make_async_copy(far_plain.at[i], far_plain_hbm.at[i], far_sems.at[2 * i]),
-                pltpu.make_async_copy(far_wind.at[i], far_wind_hbm.at[i], far_sems.at[2 * i + 1]),
-            ]
-            for copy in copies:
-                copy.start()
-            far_copies += copies
-    for copy in far_copies:
-        copy.wait()
+
+    def far_outputs(i):
+        return (
+            pltpu.make_async_copy(far_plain.at[i], far_plain_hbm.at[i], far_sems.at[2 * i]),
+            pltpu.make_async_copy(far_wind.at[i], far_wind_hbm.at[i], far_sems.at[2 * i + 1]),
+        )
+
+    @pl.loop(0, tile_count - near_count)
+    def _(i):
+        multiply(near_count + i, far_plain, far_wind, i)
+        for copy in far_outputs(i):
+            copy.start()
+
+    @pl.loop(0, near_count)
+    def _(i):
+        multiply(i, near_plain, near_wind, i)
+
+    for i in range(tile_count - near_count):
+        for copy in far_outputs(i):
+            copy.wait()
 
 
 def product(conductivity, wind, tiles, near_count):
@@ -145,27 +152,22 @@
     near_count, far_count = near_plain.shape[0], far_plain.shape[0]
     levels_n = level_weights.shape[0]
     n_lat = gathered.shape[0]
-    copies = [
-        (
+    def far_inputs(i):
+        return (
             pltpu.make_async_copy(far_plain_hbm.at[i], far_plain.at[i], sems.at[2 * i]),
             pltpu.make_async_copy(far_wind_hbm.at[i], far_wind.at[i], sems.at[2 * i + 1]),
         )
-        for i in range(far_count)
-    ]
-    for pair in copies:
-        for copy in pair:
+
+    for i in range(far_count):
+        for copy in far_inputs(i):
             copy.start()
     for level in range(levels_n):
         weights[level : level + 1, :] = jnp.full((1, COLS), level_weights[level], jnp.float32)
     plain[...] = jnp.zeros_like(plain)
     mirrored[...] = jnp.zeros_like(mirrored)
     level_of = lax.broadcasted_iota(jnp.int32, (levels_n, COLS), 0).astype(jnp.float32)
-    for k in range(near_count + far_count):
-        if k >= near_count:
-            for copy in copies[k - near_count]:
-                copy.wait()
-        near, i = k < near_count, k if k < near_count else k - near_count
-        planes = (near_plain, near_wind) if near else (far_plain, far_wind)
+
+    def integrate(k, plain_part, wind_part, i):
         target = targets[0, k]
         for row in range(ROWS):
             bounds = gathered[target, row : row + 1, :]
@@ -174,11 +176,22 @@
             inside = (level_of >= low) & (level_of < high)
             weight = jnp.where(inside, weights[...], 0.0)
             for f in range(4):
+                planes = (plain_part, wind_part)[f // 2]
                 rows = slice(f % 2 * levels_n, (f % 2 + 1) * levels_n)
-                part = planes[f // 2][i, rows, row * COLS : (row + 1) * COLS]
+                part = planes[i, rows, row * COLS : (row + 1) * COLS]
                 total = jnp.sum(part.astype(jnp.float32) * weight, axis=0, keepdims=True)
                 plain[target, f, row : row + 1, :] = total
                 mirrored[n_lat - 1 - target, f, ROWS - 1 - row : ROWS - row, :] = total
+
+    @pl.loop(0, near_count)
+    def _(i):
+        integrate(i, near_plain, near_wind, i)
+
+    @pl.loop(0, far_count)
+    def _(i):
+        for copy in far_inputs(i):
+            copy.wait()
+        integrate(near_count + i, far_plain, far_wind, i)
 
     lanes = lax.broadcasted_iota(jnp.int32, (ROWS, COLS), 1)
     for f in range(4):
@@ -242,30 +255,42 @@
         def above(blocks):
             return blocks(b + 1)[0:1] if b + 1 < n_lat else nothing
 
-        merid = combined[b, 3]
-        for f in range(3):
-            out_ref[b, f * ROWS : (f + 1) * ROWS, :] = combined[b, f]
-        out_ref[b, 24:32, :] = row_below(merid, below(lambda i: combined[i, 3])) - row_above(
-            merid, above(lambda i: combined[i, 3])
+        merid = row_below(combined[b, 3], below(lambda i: combined[i, 3])) - row_above(
+            combined[b, 3], above(lambda i: combined[i, 3])
         )
-        out_ref[b, 32:33, :] = below(lambda i: combined[i, 0])
-        out_ref[b, 33:34, :] = above(lambda i: combined[i, 0])
-        out_ref[b, 34:35, :] = below(lambda i: combined[i, 1])
-        out_ref[b, 35:36, :] = above(lambda i: combined[i, 1])
-        out_ref[b, 36:37, :] = below(lambda i: corners[i])
-        out_ref[b, 37:38, :] = above(lambda i: corners[i])
-        out_ref[b, 38:40, :] = jnp.zeros((2, COLS), jnp.float32)
+        outside = [
+            below(lambda i: combined[i, 0]),
+            above(lambda i: combined[i, 0]),
+            below(lambda i: combined[i, 1]),
+            above(lambda i: combined[i, 1]),
+            below(lambda i: corners[i]),
+            above(lambda i: corners[i]),
+            nothing,
+            nothing,
+        ]
         columns = jnp.zeros((ROWS, COLS), jnp.float32)
         for f in range(3):
             moved = pltpu.roll(beyond[f], (COLS + 2 * f - 2 * b) % COLS, 1)
             columns = jnp.where((lanes >= 2 * f) & (lanes < 2 * f + 2), moved, columns)
-        out_ref[b, 40:48, :] = columns
+
+        def put(start, *blocks):
+            out_ref[b, start : start + 2 * ROWS, :] = jnp.concatenate(blocks, 0).astype(jnp.bfloat16)
+
+        put(0, combined[b, 0], combined[b, 1])
+        put(16, *both_parts(combined[b, 2]))
+        put(32, *both_parts(merid))
+        put(48, *outside, columns)
+
+
+def both_parts(block):
+    first = block.astype(jnp.bfloat16).astype(jnp.float32)
+    return first, block - first
 
 
 def assemble(combined, inside, across):
     return pl.pallas_call(
         assemble_kernel,
-        out_shape=jax.ShapeDtypeStruct((combined.shape[0], SUM_ROWS, COLS), jnp.float32),
+        out_shape=jax.ShapeDtypeStruct((combined.shape[0], SUM_ROWS, COLS), jnp.bfloat16),
         in_specs=[VMEM_SPEC] * 3,
         out_specs=VMEM_SPEC,
         compiler_params=pltpu.CompilerParams(vmem_limit_bytes=SMALL),
@@ -335,11 +360,10 @@
 
 
 def stencil_kernel(received, stencil_ref, source_ref):
-    sums = received[0]
+    sums = received[0].astype(jnp.float32)
     for source in range(1, received.shape[0]):
-        sums += received[source]
+        sums += received[source].astype(jnp.float32)
     lanes = lax.broadcasted_iota(jnp.int32, (ROWS, COLS), 1)
-    columns = sums[40:48]
 
     def eastward(block, beyond, lane):
         moved = pltpu.roll(beyond, COLS - 1 - lane, 1)
@@ -349,7 +373,10 @@
         moved = pltpu.roll(beyond, (COLS - lane) % COLS, 1)
         return jnp.where(lanes == 0, moved, pltpu.roll(block, 1, 1))
 
-    center0, center1, zonal, merid, edge = (sums[i * ROWS : (i + 1) * ROWS] for i in range(5))
+    center0, center1, zonal, zonal_left, merid, merid_left, edge, columns = (
+        sums[i * ROWS : (i + 1) * ROWS] for i in range(8)
+    )
+    zonal, merid = zonal + zonal_left, merid + merid_left
     corner = pltpu.roll(edge, ROWS - 2, 0)
     edge_east, edge_west = eastward(edge, corner, 0), westward(edge, corner, 1)
     east1, west1 = eastward(center1, columns, 2), westward(center1, columns, 3)

time: 44.2 us -> 43.5 us (0.984)
  waiting for transfers between devices: 4.06 us -> 3.36 us
    all_to_all x1, waiting for transfers between devices: 1.86 us -> 1.16 us  [per_device(): received = lax.all_to_all(sends, 'lat', 0, 0, tiled=True)]
  transfers between devices with their start and end apart: 4 -> 4, of which waited for: 2 -> 2; matrix products, arithmetic and copies ran while one was open for 0% -> 0% of each run, Pallas kernels for 36% -> 37%
where the time goes in v4:
time: 43.5 us; the launch traced here: 43.1 us
  Pallas kernels  21.6 us (50%)
  starting transfers between devices  17.4 us (40%)
  waiting for transfers between devices  3.36 us (8%)
  between operations  0.71 us (2%)
    pallas_call x1, Pallas kernels, product(): pl.pallas_call(product_kernel, out_shape=(pltpu.VMEM(near_shape, jnp.bflo...  8.3 us
    all_to_all x1, starting transfers between devices, per_device(): gathered = lax.all_to_all(packed, 'lat', 0, 0, tiled=True)  7.96 us
    pallas_call x1, Pallas kernels, backward(): pl.pallas_call(backward_kernel, out_shape=jax.ShapeDtypeStruct((2, geo_ce...  7.53 us
    all_to_all x1, starting transfers between devices, per_device(): received = lax.all_to_all(sends, 'lat', 0, 0, tiled=True)  7.21 us
    pallas_call x1, Pallas kernels, integral(): pl.pallas_call(integral_kernel, out_shape=(pltpu.VMEM((n_lat, 4, ROWS, CO...  2.81 us
    ppermute x1, starting transfers between devices, lon_neighbours(): lax.ppermute(block, 'lon', across)  2.25 us
    ppermute x1, waiting for transfers between devices, lon_neighbours(): lax.ppermute(block, 'lon', across)  2.2 us
    pallas_call x1, Pallas kernels, pack(): pl.pallas_call(pack_kernel, out_shape=pltpu.VMEM((n_lat, 2 * ROWS, COLS),...  1.37 us
  transfers between devices with their start and end apart: 4, of which 2 were waited for; matrix products, arithmetic and copies ran while one was open for 0% of the time, Pallas kernels for 37%

profile of v4, /device:TPU:0, one launch (start us, length us, event | category | flops | bytes accessed | tf_op | source)
XLA Modules:
  0.0 43.1 jit_solution(9843515901769196014)
XLA Ops:
  0.6 1.4 %pack_levels_potential.1 = f32[16,16,128]{2,1,0:T(8,128)} custom-call(s32[2,8,128]{2,1,0:T(8,128)} %levels_ref.1, f32[8,128]{1,0:T(8,128)} %potential_ref.1), custom_call_target="tpu_custom_call" | custom-call | tf_op jit(solution)/shard_map/pack_levels_potential/pallas_call | solution.py:30
  2.0 8.0 %all-to-all-start = ((f32[16,16,128]{2,1,0:T(8,128)}), f32[16,16,128]{2,1,0:T(8,128)S(1)}, u32[]{:S(2)}, u32[]{:S(2)}) async-start(f32[16,16,128]{2,1,0:T(8,128)} %pack_levels_potential.1), calls=%async_computation | async-start | bytes 262144 | tf_op jit(solution)/shard_map/all_to_all | solution.py:433
  10.0 0.0 copy-start
  10.0 0.0 copy-start.1
  10.0 8.3 %regrid_product.1 = (bf16[4,128,1024]{2,1,0:T(8,128)(2,1)S(1)}, f32[4,128,1024]{2,1,0:T(8,128)S(1)}, bf16[4,128,1024]{2,1,0:T(8,128)(2,1)}, f32[4,128,1024]{2,1,0:T(8,128)}) custom-call(bf16[2,64,1024]{2,1,0:T(8,128)(2,1)} %conductivity_hbm.1, bf16[4,64,1024]{2,1,0:T(8,128)(2,1)} %wind_hbm.1, bf16[8,1024,1024]{2,1,0:T(8,128)(2,1)} %tiles_hbm.3), custom_call_target="tpu_custom_call" | custom-call | flops 4294967296 | bytes 16777216 | tf_op jit(solution)/shard_map/regrid_product/pallas_call | solution.py:120
  18.3 0.0 all-to-all-done.gathered
  18.3 0.0 copy-done
  18.3 0.0 copy-done.1
  18.3 2.8 %level_integral.1 = (f32[16,4,8,128]{3,2,1,0:T(8,128)S(1)}, f32[32,128]{1,0:T(8,128)S(1)}) custom-call(s32[1,8]{1,0:T(1,128)S(1)} %copy-done, f32[64]{0:T(128)S(1)} %copy-done.1, f32[16,16,128]{2,1,0:T(8,128)S(1)} %all-to-all-done.gathered, bf16[4,128,1024]{2,1,0:T(8,128)(2,1)S(1)} %get-tuple-element.11.near_plain, ...), custom_call_target="tpu_custom_call" | custom-call | flops 3145728 | bytes 8388608 | tf_op jit(solution)/shard_map/level_integral/pallas_call | solution.py:217
  21.1 2.3 %collective-permute-start.1 = (f32[32,128]{1,0:T(8,128)S(1)}, f32[32,128]{1,0:T(8,128)S(1)}, u32[]{:S(2)}, u32[]{:S(2)}) collective-permute-start(f32[32,128]{1,0:T(8,128)S(1)} %get-tuple-element.16), channel_id=1, source_target_pairs={{0,7},{1,2},{2,1},{3,4},{4,3},{5,6},{6,5},{7,0},{8,15},{9,10},{10,... | collective-permute-start | bytes 49160 | tf_op jit(solution)/shard_map/ppermute | solution.py:418
  23.4 0.0 collective-permute-start
  23.4 2.2 %collective-permute-done.1.across = f32[32,128]{1,0:T(8,128)S(1)} collective-permute-done((f32[32,128]{1,0:T(8,128)S(1)}, f32[32,128]{1,0:T(8,128)S(1)}, u32[]{:S(2)}, u32[]{:S(2)}) %collective-permute-start.1) | collective-permute-done | bytes 16416 | tf_op jit(solution)/shard_map/ppermute | solution.py:418
  25.6 0.0 collective-permute-done.inside
  25.6 0.8 %assemble_sends.1 = bf16[16,64,128]{2,1,0:T(8,128)(2,1)} custom-call(f32[16,4,8,128]{3,2,1,0:T(8,128)S(1)} %get-tuple-element.15.combined, f32[32,128]{1,0:T(8,128)S(1)} %collective-permute-done.inside, f32[32,128]{1,0:T(8,128)S(1)} %collective-permute-done.1.across), custom_call_target="tpu_custom_call" | custom-call | tf_op jit(solution)/shard_map/assemble_sends/pallas_call | solution.py:291
  26.4 7.2 %all-to-all-start.1 = ((bf16[16,64,128]{2,1,0:T(8,128)(2,1)}), bf16[16,64,128]{2,1,0:T(8,128)(2,1)S(1)}, u32[]{:S(2)}, u32[]{:S(2)}) async-start(bf16[16,64,128]{2,1,0:T(8,128)(2,1)} %assemble_sends.1), calls=%async_computation.1 | async-start | bytes 524288 | tf_op jit(solution)/shard_map/all_to_all | solution.py:438
  33.7 7.5 %electric_to_geo.1 = f32[2,1024]{1,0:T(2,128)} custom-call(s32[1,8]{1,0:T(1,128)S(1)} %copy-done, f32[16,16,128]{2,1,0:T(8,128)S(1)} %all-to-all-done.gathered, f32[32,128]{1,0:T(8,128)S(1)} %collective-permute-done.inside, f32[32,128]{1,0:T(8,128)S(1)} %collective-permute-done.1.across, bf16[8,1024,1024]{2,1,0:T(8,128)(2,1)} %tiles_hbm.3), custom_call_target="tpu_custom_call" | custom-call | flops 134217728 | bytes 16777216 | tf_op jit(solution)/shard_map/electric_to_geo/pallas_call | solution.py:342
  41.2 1.2 %all-to-all-done.1.received = bf16[16,64,128]{2,1,0:T(8,128)(2,1)S(1)} async-done(((bf16[16,64,128]{2,1,0:T(8,128)(2,1)}), bf16[16,64,128]{2,1,0:T(8,128)(2,1)S(1)}, u32[]{:S(2)}, u32[]{:S(2)}) %all-to-all-start.1) | async-done | bytes 262176 | tf_op jit(solution)/shard_map/all_to_all | solution.py:438
  42.3 0.7 %stencil_source.1 = (f32[9,8,128]{2,1,0:T(8,128)}, f32[8,128]{1,0:T(8,128)}) custom-call(bf16[16,64,128]{2,1,0:T(8,128)(2,1)S(1)} %all-to-all-done.1.received), custom_call_target="tpu_custom_call" | custom-call | tf_op jit(solution)/shard_map/stencil_source/pallas_call | solution.py:401
Async XLA Ops:
  2.0 16.3 %all-to-all-start = ((f32[16,16,128]{2,1,0:T(8,128)}), f32[16,16,128]{2,1,0:T(8,128)S(1)}, u32[]{:S(2)}, u32[]{:S(2)}) async-start(f32[16,16,128]{2,1,0:T(8,128)} %pack_levels_potential.1), calls=%async_computation | async-start | bytes 262144 | tf_op jit(solution)/shard_map/all_to_all | solution.py:433
  10.0 8.3 %copy-start = (s32[1,8]{1,0:T(1,128)S(1)}, s32[1,8]{1,0:T(1,128)}, u32[]{:S(2)}) copy-start(s32[1,8]{1,0:T(1,128)} %targets.3) | copy-start | bytes 100
  10.0 8.3 %copy-start.1 = (f32[64]{0:T(128)S(1)}, f32[64]{0:T(128)}, u32[]{:S(2)}) copy-start(f32[64]{0:T(128)} %level_weights.1) | copy-start | bytes 772
  21.1 4.5 %collective-permute-start.1 = (f32[32,128]{1,0:T(8,128)S(1)}, f32[32,128]{1,0:T(8,128)S(1)}, u32[]{:S(2)}, u32[]{:S(2)}) collective-permute-start(f32[32,128]{1,0:T(8,128)S(1)} %get-tuple-element.16), channel_id=1, source_target_pairs={{0,7},{1,2},{2,1},{3,4},{4,3},{5,6},{6,5},{7,0},{8,15},{9,10},{10,... | collective-permute-start | bytes 49160 | tf_op jit(solution)/shard_map/ppermute | solution.py:418
  23.4 2.2 %collective-permute-start = (f32[32,128]{1,0:T(8,128)S(1)}, f32[32,128]{1,0:T(8,128)S(1)}, u32[]{:S(2)}, u32[]{:S(2)}) collective-permute-start(f32[32,128]{1,0:T(8,128)S(1)} %get-tuple-element.16), channel_id=1, source_target_pairs={{0,1},{1,0},{2,3},{3,2},{4,5},{5,4},{6,7},{7,6},{8,9},{9,8},{10,11... | collective-permute-start | bytes 49160 | tf_op jit(solution)/shard_map/ppermute | solution.py:418
  26.4 15.9 %all-to-all-start.1 = ((bf16[16,64,128]{2,1,0:T(8,128)(2,1)}), bf16[16,64,128]{2,1,0:T(8,128)(2,1)S(1)}, u32[]{:S(2)}, u32[]{:S(2)}) async-start(bf16[16,64,128]{2,1,0:T(8,128)(2,1)} %assemble_sends.1), calls=%async_computation.1 | async-start | bytes 524288 | tf_op jit(solution)/shard_map/all_to_all | solution.py:438

commit v5 on v4

--- a/solution.py
+++ b/solution.py
@@ -13,6 +13,7 @@
 SCOPED = 24 * 2**20
 SMALL = 8 * 2**20
 CHUNK = 2 * COLS
+FAR_TILES = 2
 VMEM_SPEC = pl.BlockSpec(memory_space=pltpu.VMEM)
 HBM_SPEC = pl.BlockSpec(memory_space=pltpu.HBM)
 SMEM_SPEC = pl.BlockSpec(memory_space=pltpu.SMEM)
@@ -50,26 +51,31 @@
     return pltpu.with_memory_space_constraint(array, pltpu.VMEM)
 
 
+def in_smem(array):
+    return pltpu.with_memory_space_constraint(array, pltpu.SMEM)
+
+
 def in_hbm(array):
     return pltpu.with_memory_space_constraint(array, pltpu.HBM)
 
 
 def product_kernel(
-    conductivity_hbm, wind_hbm, tiles_hbm, near_plain, near_wind, far_plain_hbm, far_wind_hbm,
-    fields, conductivity, wind, tiles, far_plain, far_wind, sems, far_sems,
+    conductivity_hbm, wind_hbm, tiles_hbm, near_plain, near_zonal, near_merid, far_plain_hbm, far_zonal_hbm, far_merid_hbm,
+    fields, conductivity, wind, tiles, far_plain, far_zonal, far_merid, sems, far_sems,
 ):
     tile_count, mag_cells, geo_cells = tiles.shape
     levels_n = conductivity.shape[1]
     near_count = near_plain.shape[0]
     order = list(range(near_count, tile_count)) + list(range(near_count))
+    far_merid_count = far_merid.shape[0]
     field_copies = [
         pltpu.make_async_copy(conductivity_hbm, conductivity, sems.at[tile_count]),
         pltpu.make_async_copy(wind_hbm, wind, sems.at[tile_count + 1]),
     ]
-    def tile_copy(k):
-        return pltpu.make_async_copy(tiles_hbm.at[k], tiles.at[k], sems.at[k])
-
-    for copy in field_copies + [tile_copy(k) for k in order]:
+    tile_copies = {
+        k: pltpu.make_async_copy(tiles_hbm.at[k], tiles.at[k], sems.at[k]) for k in order
+    }
+    for copy in field_copies + [tile_copies[k] for k in order]:
         copy.start()
     for copy in field_copies:
         copy.wait()
@@ -78,8 +84,18 @@
     first, second, third, fourth = (wind[i].astype(jnp.float32) for i in range(4))
     fields[2 * levels_n : 3 * levels_n, :] = (third - second).astype(jnp.bfloat16)
     fields[3 * levels_n : 4 * levels_n, :] = (first + fourth).astype(jnp.bfloat16)
-    def multiply(k, plain_out, wind_out, i):
-        tile_copy(k).wait()
+    outputs = []
+
+    def send(source, target):
+        copy = pltpu.make_async_copy(source, target, far_sems.at[len(outputs)])
+        copy.start()
+        outputs.append(copy)
+
+    for step, k in enumerate(order):
+        tile_copies[k].wait()
+        near, i = k < near_count, k if k < near_count else k - near_count
+        plain_out, zonal_out = (near_plain, near_zonal) if near else (far_plain, far_zonal)
+        merid_out, m = (far_merid, step) if step < far_merid_count else (near_merid, step - far_merid_count)
         for start in range(0, mag_cells, CHUNK):
             columns = slice(start, start + CHUNK)
             value = lax.dot_general(
@@ -89,53 +105,45 @@
                 preferred_element_type=jnp.float32,
             )
             plain_out[i, :, columns] = value[: 2 * levels_n].astype(jnp.bfloat16)
-            wind_out[i, :, columns] = value[2 * levels_n :]
-
-    def far_outputs(i):
-        return (
-            pltpu.make_async_copy(far_plain.at[i], far_plain_hbm.at[i], far_sems.at[2 * i]),
-            pltpu.make_async_copy(far_wind.at[i], far_wind_hbm.at[i], far_sems.at[2 * i + 1]),
-        )
-
-    @pl.loop(0, tile_count - near_count)
-    def _(i):
-        multiply(near_count + i, far_plain, far_wind, i)
-        for copy in far_outputs(i):
-            copy.start()
-
-    @pl.loop(0, near_count)
-    def _(i):
-        multiply(i, near_plain, near_wind, i)
-
-    for i in range(tile_count - near_count):
-        for copy in far_outputs(i):
-            copy.wait()
+            zonal_out[i, :, columns] = value[2 * levels_n : 3 * levels_n]
+            merid_out[m, :, columns] = value[3 * levels_n :]
+        if not near:
+            send(far_plain.at[i], far_plain_hbm.at[i])
+            send(far_zonal.at[i], far_zonal_hbm.at[i])
+        if step < far_merid_count:
+            send(far_merid.at[m], far_merid_hbm.at[m])
+    for copy in outputs:
+        copy.wait()
 
 
 def product(conductivity, wind, tiles, near_count):
     levels_n, geo_cells = conductivity.shape[1:]
     tile_count, mag_cells = tiles.shape[:2]
     far_count = tile_count - near_count
-    near_shape, far_shape = ((count, 2 * levels_n, mag_cells) for count in (near_count, far_count))
+    plain = lambda count: ((count, 2 * levels_n, mag_cells), jnp.bfloat16)
+    wind_term = lambda count: ((count, levels_n, mag_cells), jnp.float32)
     return pl.pallas_call(
         product_kernel,
         out_shape=(
-            pltpu.VMEM(near_shape, jnp.bfloat16),
-            pltpu.VMEM(near_shape, jnp.float32),
-            pltpu.HBM(far_shape, jnp.bfloat16),
-            pltpu.HBM(far_shape, jnp.float32),
+            pltpu.VMEM(*plain(near_count)),
+            pltpu.VMEM(*wind_term(near_count)),
+            pltpu.VMEM(*wind_term(1)),
+            pltpu.HBM(*plain(far_count)),
+            pltpu.HBM(*wind_term(far_count)),
+            pltpu.HBM(*wind_term(tile_count - 1)),
         ),
         in_specs=[HBM_SPEC] * 3,
-        out_specs=(VMEM_SPEC, VMEM_SPEC, HBM_SPEC, HBM_SPEC),
+        out_specs=(VMEM_SPEC,) * 3 + (HBM_SPEC,) * 3,
         scratch_shapes=[
             pltpu.VMEM((4 * levels_n, geo_cells), jnp.bfloat16),
             pltpu.VMEM(conductivity.shape, conductivity.dtype),
             pltpu.VMEM(wind.shape, wind.dtype),
             pltpu.VMEM(tiles.shape, tiles.dtype),
-            pltpu.VMEM(far_shape, jnp.bfloat16),
-            pltpu.VMEM(far_shape, jnp.float32),
+            pltpu.VMEM(*plain(far_count)),
+            pltpu.VMEM(*wind_term(far_count)),
+            pltpu.VMEM(*wind_term(tile_count - 1)),
             pltpu.SemaphoreType.DMA((tile_count + 2,)),
-            pltpu.SemaphoreType.DMA((2 * far_count,)),
+            pltpu.SemaphoreType.DMA((2 * far_count + tile_count - 1,)),
         ],
         compiler_params=pltpu.CompilerParams(vmem_limit_bytes=SCOPED),
         cost_estimate=pl.CostEstimate(
@@ -145,58 +153,70 @@
     )(conductivity, wind, tiles)
 
 
+def masked_weights(target, row, gathered, weights):
+    levels_n = weights.shape[0]
+    level_of = lax.broadcasted_iota(jnp.int32, (levels_n, COLS), 0).astype(jnp.float32)
+    bounds = gathered[target, row : row + 1, :]
+    low = jnp.floor(bounds * (1.0 / RADIX))
+    high = bounds - low * RADIX
+    inside = (level_of >= low) & (level_of < high)
+    return jnp.where(inside, weights[...], 0.0)
+
+
+def fill_weights(level_weights, weights):
+    for level in range(weights.shape[0]):
+        weights[level : level + 1, :] = jnp.full((1, COLS), level_weights[level], jnp.float32)
+
+
 def integral_kernel(
-    targets, level_weights, gathered, near_plain, near_wind, far_plain_hbm, far_wind_hbm, combined, edges,
-    weights, plain, mirrored, far_plain, far_wind, sems,
+    targets, level_weights, gathered, near_plain, near_zonal, far_plain_hbm, far_zonal_hbm, combined, edges,
+    weights, plain, mirrored, far_plain, far_zonal, sems,
 ):
     near_count, far_count = near_plain.shape[0], far_plain.shape[0]
     levels_n = level_weights.shape[0]
     n_lat = gathered.shape[0]
+
     def far_inputs(i):
         return (
             pltpu.make_async_copy(far_plain_hbm.at[i], far_plain.at[i], sems.at[2 * i]),
-            pltpu.make_async_copy(far_wind_hbm.at[i], far_wind.at[i], sems.at[2 * i + 1]),
+            pltpu.make_async_copy(far_zonal_hbm.at[i], far_zonal.at[i], sems.at[2 * i + 1]),
         )
 
     for i in range(far_count):
         for copy in far_inputs(i):
             copy.start()
-    for level in range(levels_n):
-        weights[level : level + 1, :] = jnp.full((1, COLS), level_weights[level], jnp.float32)
+    fill_weights(level_weights, weights)
     plain[...] = jnp.zeros_like(plain)
     mirrored[...] = jnp.zeros_like(mirrored)
-    level_of = lax.broadcasted_iota(jnp.int32, (levels_n, COLS), 0).astype(jnp.float32)
-
-    def integrate(k, plain_part, wind_part, i):
+
+    def integrate(k, plain_part, zonal_part, i):
         target = targets[0, k]
+        opposite = n_lat - 1 - target
         for row in range(ROWS):
-            bounds = gathered[target, row : row + 1, :]
-            low = jnp.floor(bounds * (1.0 / RADIX))
-            high = bounds - low * RADIX
-            inside = (level_of >= low) & (level_of < high)
-            weight = jnp.where(inside, weights[...], 0.0)
-            for f in range(4):
-                planes = (plain_part, wind_part)[f // 2]
-                rows = slice(f % 2 * levels_n, (f % 2 + 1) * levels_n)
-                part = planes[i, rows, row * COLS : (row + 1) * COLS]
+            columns = slice(row * COLS, (row + 1) * COLS)
+            weight = masked_weights(target, row, gathered, weights)
+            for f in range(3):
+                planes = zonal_part if f == 2 else plain_part
+                start = 0 if f == 2 else f * levels_n
+                part = planes[i, start : start + levels_n, columns]
                 total = jnp.sum(part.astype(jnp.float32) * weight, axis=0, keepdims=True)
-                plain[target, f, row : row + 1, :] = total
-                mirrored[n_lat - 1 - target, f, ROWS - 1 - row : ROWS - row, :] = total
+                plain[target, f * ROWS + row : f * ROWS + row + 1, :] = total
+                last = (f + 1) * ROWS - 1 - row
+                mirrored[opposite, last : last + 1, :] = total
 
     @pl.loop(0, near_count)
     def _(i):
-        integrate(i, near_plain, near_wind, i)
+        integrate(i, near_plain, near_zonal, i)
 
     @pl.loop(0, far_count)
     def _(i):
         for copy in far_inputs(i):
             copy.wait()
-        integrate(near_count + i, far_plain, far_wind, i)
+        integrate(near_count + i, far_plain, far_zonal, i)
 
     lanes = lax.broadcasted_iota(jnp.int32, (ROWS, COLS), 1)
-    for f in range(4):
-        for b in range(n_lat):
-            combined[b, f] = plain[b, f] + mirrored[b, f]
+    for b in range(n_lat):
+        combined[b] = plain[b] + mirrored[b]
 
     def both_edges(block_of):
         edge = jnp.zeros((ROWS, COLS), jnp.float32)
@@ -207,38 +227,103 @@
         return edge
 
     for f in range(3):
-        edges[f * ROWS : (f + 1) * ROWS, :] = both_edges(lambda b: combined[b, f])
+        rows = slice(f * ROWS, (f + 1) * ROWS)
+        edges[rows, :] = both_edges(lambda b: combined[b, rows, :])
     edges[3 * ROWS : 4 * ROWS, :] = both_edges(lambda b: gathered[b, ROWS : 2 * ROWS, :])
 
 
 def integral(targets, level_weights, gathered, near, far):
-    far_shape = far[0].shape
+    far_count = far[0].shape[0]
+    levels_n = level_weights.shape[0]
     n_lat = gathered.shape[0]
     return pl.pallas_call(
         integral_kernel,
         out_shape=(
-            pltpu.VMEM((n_lat, 4, ROWS, COLS), jnp.float32),
+            pltpu.VMEM((n_lat, 3 * ROWS, COLS), jnp.float32),
             pltpu.VMEM((4 * ROWS, COLS), jnp.float32),
         ),
         in_specs=[SMEM_SPEC] * 2 + [VMEM_SPEC] * 3 + [HBM_SPEC] * 2,
         out_specs=(VMEM_SPEC, VMEM_SPEC),
         scratch_shapes=[
-            pltpu.VMEM((level_weights.shape[0], COLS), jnp.float32),
-            pltpu.VMEM((n_lat, 4, ROWS, COLS), jnp.float32),
-            pltpu.VMEM((n_lat, 4, ROWS, COLS), jnp.float32),
-            pltpu.VMEM(far_shape, jnp.bfloat16),
-            pltpu.VMEM(far_shape, jnp.float32),
-            pltpu.SemaphoreType.DMA((2 * far_shape[0],)),
+            pltpu.VMEM((levels_n, COLS), jnp.float32),
+            pltpu.VMEM((n_lat, 3 * ROWS, COLS), jnp.float32),
+            pltpu.VMEM((n_lat, 3 * ROWS, COLS), jnp.float32),
+            pltpu.VMEM(far[0].shape, far[0].dtype),
+            pltpu.VMEM(far[1].shape, far[1].dtype),
+            pltpu.SemaphoreType.DMA((2 * far_count,)),
         ],
         compiler_params=pltpu.CompilerParams(vmem_limit_bytes=SCOPED),
         cost_estimate=pl.CostEstimate(
             flops=6 * near[0].size, bytes_accessed=16 * near[0].size, transcendentals=0
         ),
         name="level_integral",
-    )(targets, level_weights, in_vmem(gathered), *map(in_vmem, near), *map(in_hbm, far))
-
-
-def assemble_kernel(combined, inside, across, out_ref):
+    )(in_smem(targets), in_smem(level_weights), in_vmem(gathered), *map(in_vmem, near), *map(in_hbm, far))
+
+
+def meridional_kernel(
+    targets, level_weights, gathered, near, far_hbm, out_ref, weights, total, far, sems
+):
+    far_count = far.shape[0]
+    tile_count = targets.shape[1]
+    levels_n = level_weights.shape[0]
+    n_lat = gathered.shape[0]
+    shift = tile_count - FAR_TILES
+
+    def far_input(i):
+        return pltpu.make_async_copy(far_hbm.at[i], far.at[i], sems.at[i])
+
+    for i in range(far_count):
+        far_input(i).start()
+    fill_weights(level_weights, weights)
+    total[...] = jnp.zeros_like(total)
+
+    def integrate(step, planes, i):
+        target = targets[0, lax.rem(step + shift, tile_count)]
+        for row in range(ROWS):
+            columns = slice(row * COLS, (row + 1) * COLS)
+            weight = masked_weights(target, row, gathered, weights)
+            value = jnp.sum(planes[i, :, columns] * weight, axis=0, keepdims=True)
+            total[0, target, row : row + 1, :] = value
+            total[1, n_lat - 1 - target, ROWS - 1 - row : ROWS - row, :] = value
+
+    integrate(far_count, near, 0)
+
+    @pl.loop(0, far_count)
+    def _(i):
+        far_input(i).wait()
+        integrate(i, far, i)
+
+    merid = [total[0, b] + total[1, b] for b in range(n_lat)]
+    nothing = jnp.zeros((1, COLS), jnp.float32)
+    for b in range(n_lat):
+        below = merid[b - 1][ROWS - 1 : ROWS] if b > 0 else nothing
+        above = merid[b + 1][0:1] if b + 1 < n_lat else nothing
+        out_ref[b] = row_below(merid[b], below) - row_above(merid[b], above)
+
+
+def meridional(targets, level_weights, gathered, near, far):
+    n_lat = gathered.shape[0]
+    levels_n = level_weights.shape[0]
+    return pl.pallas_call(
+        meridional_kernel,
+        out_shape=pltpu.VMEM((n_lat, ROWS, COLS), jnp.float32),
+        in_specs=[SMEM_SPEC] * 2 + [VMEM_SPEC] * 2 + [HBM_SPEC],
+        out_specs=VMEM_SPEC,
+        scratch_shapes=[
+            pltpu.VMEM((levels_n, COLS), jnp.float32),
+            pltpu.VMEM((2, n_lat, ROWS, COLS), jnp.float32),
+            pltpu.VMEM(far.shape, far.dtype),
+            pltpu.SemaphoreType.DMA((far.shape[0],)),
+        ],
+        compiler_params=pltpu.CompilerParams(vmem_limit_bytes=SCOPED),
+        cost_estimate=pl.CostEstimate(
+            flops=4 * far.size, bytes_accessed=8 * far.size, transcendentals=0
+        ),
+        name="meridional_integral",
+    )(in_smem(targets), in_smem(level_weights), in_vmem(gathered), in_vmem(near), in_hbm(far))
+
+
+def assemble_kernel(combined, merid, inside, across, out_ref):
     n_lat = combined.shape[0]
     lanes = lax.broadcasted_iota(jnp.int32, (ROWS, COLS), 1)
     beyond = []
@@ -255,14 +340,11 @@
         def above(blocks):
             return blocks(b + 1)[0:1] if b + 1 < n_lat else nothing
 
-        merid = row_below(combined[b, 3], below(lambda i: combined[i, 3])) - row_above(
-            combined[b, 3], above(lambda i: combined[i, 3])
-        )
         outside = [
-            below(lambda i: combined[i, 0]),
-            above(lambda i: combined[i, 0]),
-            below(lambda i: combined[i, 1]),
-            above(lambda i: combined[i, 1]),
+            below(lambda i: combined[i, 0:8]),
+            above(lambda i: combined[i, 0:8]),
+            below(lambda i: combined[i, 8:16]),
+            above(lambda i: combined[i, 8:16]),
             below(lambda i: corners[i]),
             above(lambda i: corners[i]),
             nothing,
@@ -276,9 +358,9 @@
         def put(start, *blocks):
             out_ref[b, start : start + 2 * ROWS, :] = jnp.concatenate(blocks, 0).astype(jnp.bfloat16)
 
-        put(0, combined[b, 0], combined[b, 1])
-        put(16, *both_parts(combined[b, 2]))
-        put(32, *both_parts(merid))
+        put(0, combined[b, 0:8], combined[b, 8:16])
+        put(16, *both_parts(combined[b, 16:24]))
+        put(32, *both_parts(merid[b]))
         put(48, *outside, columns)
 
 
@@ -287,15 +369,15 @@
     return first, block - first
 
 
-def assemble(combined, inside, across):
+def assemble(combined, merid, inside, across):
     return pl.pallas_call(
         assemble_kernel,
         out_shape=jax.ShapeDtypeStruct((combined.shape[0], SUM_ROWS, COLS), jnp.bfloat16),
-        in_specs=[VMEM_SPEC] * 3,
+        in_specs=[VMEM_SPEC] * 4,
         out_specs=VMEM_SPEC,
         compiler_params=pltpu.CompilerParams(vmem_limit_bytes=SMALL),
         name="assemble_sends",
-    )(in_vmem(combined), in_vmem(inside), in_vmem(across))
+    )(in_vmem(combined), in_vmem(merid), in_vmem(inside), in_vmem(across))
 
 
 def backward_kernel(targets, gathered, inside, across, tiles_hbm, out_ref, zonal, merid, rows_ref, tiles, sems):
@@ -356,7 +438,7 @@
             flops=16 * tiles.size, bytes_accessed=2 * tiles.size, transcendentals=0
         ),
         name="electric_to_geo",
-    )(targets, in_vmem(gathered), in_vmem(inside), in_vmem(across), tiles)
+    )(in_smem(targets), in_vmem(gathered), in_vmem(inside), in_vmem(across), tiles)
 
 
 def stencil_kernel(received, stencil_ref, source_ref):
@@ -428,13 +510,18 @@
 ):
     n_lat = lax.axis_size("lat")
     tiles = in_hbm(correlation_tiles)
-    near_count = tiles.shape[0] // 2
     packed = pack(line_levels, potential, n_lat)
     gathered = lax.all_to_all(packed, "lat", 0, 0, tiled=True)
-    near_plain, near_wind, far_plain, far_wind = product(in_hbm(conductivity), in_hbm(wind_terms), tiles, near_count)
-    combined, edges = integral(tile_targets, level_weights, gathered, (near_plain, near_wind), (far_plain, far_wind))
+    near_plain, near_zonal, near_merid, far_plain, far_zonal, far_merid = product(
+        in_hbm(conductivity), in_hbm(wind_terms), tiles, tiles.shape[0] - FAR_TILES
+    )
+    combined, edges = integral(
+        tile_targets, level_weights, gathered, (near_plain, near_zonal), (far_plain, far_zonal)
+    )
+    edges, near_merid = lax.optimization_barrier((edges, near_merid))
     inside, across = lon_neighbours(edges)
-    sends = assemble(combined, inside, across)
+    merid = meridional(tile_targets, level_weights, gathered, near_merid, far_merid)
+    sends = assemble(combined, merid, inside, across)
     received = lax.all_to_all(sends, "lat", 0, 0, tiled=True)
     geo_field = backward(tile_targets, gathered, inside, across, tiles)
     stencil, source_term = stencil_source(received)

time: 43.5 us -> 42.9 us (0.986)
  waiting for transfers between devices: 3.36 us -> 1.56 us
  Pallas kernels: 21.6 us -> 22.7 us
    ppermute x1, waiting for transfers between devices: 2.2 us -> 0.04 us  [lon_neighbours(): lax.ppermute(block, 'lon', across)]
    pallas_call x2 -> x3, Pallas kernels: 11.1 us -> 12.3 us  [the longest x1 8.05 us: product(): pl.pallas_call(product_kernel, out_shape=(pltpu.VMEM(*plain(near_count)),...]
  transfers between devices with their start and end apart: 4 -> 4, of which waited for: 2 -> 1; matrix products, arithmetic and copies ran while one was open for 0% -> 0% of each run, Pallas kernels for 37% -> 42%
where the time goes in v5:
time: 42.9 us; the launch traced here: 42.5 us
  Pallas kernels  22.7 us (53%)
  starting transfers between devices  17.4 us (41%)
  waiting for transfers between devices  1.56 us (4%)
  between operations  0.72 us (2%)
    pallas_call x1, Pallas kernels, product(): pl.pallas_call(product_kernel, out_shape=(pltpu.VMEM(*plain(near_count)),...  8.05 us
    all_to_all x1, starting transfers between devices, per_device(): gathered = lax.all_to_all(packed, 'lat', 0, 0, tiled=True)  7.96 us
    pallas_call x1, Pallas kernels, backward(): pl.pallas_call(backward_kernel, out_shape=jax.ShapeDtypeStruct((2, geo_ce...  7.53 us
    all_to_all x1, starting transfers between devices, per_device(): received = lax.all_to_all(sends, 'lat', 0, 0, tiled=True)  7.22 us
    ppermute x1, starting transfers between devices, lon_neighbours(): lax.ppermute(block, 'lon', across)  2.26 us
    pallas_call x1, Pallas kernels, meridional(): pl.pallas_call(meridional_kernel, out_shape=pltpu.VMEM((n_lat, ROWS, COLS...  2.14 us
    pallas_call x1, Pallas kernels, integral(): pl.pallas_call(integral_kernel, out_shape=(pltpu.VMEM((n_lat, 3 * ROWS, C...  2.1 us
    all_to_all x1, waiting for transfers between devices, per_device(): received = lax.all_to_all(sends, 'lat', 0, 0, tiled=True)  1.51 us
  transfers between devices with their start and end apart: 4, of which 1 were waited for; matrix products, arithmetic and copies ran while one was open for 0% of the time, Pallas kernels for 42%

profile of v5, /device:TPU:0, one launch (start us, length us, event | category | flops | bytes accessed | tf_op | source)
XLA Modules:
  0.0 42.5 jit_solution(13927555396031194319)
XLA Ops:
  0.6 1.4 %pack_levels_potential.1 = f32[16,16,128]{2,1,0:T(8,128)} custom-call(s32[2,8,128]{2,1,0:T(8,128)} %levels_ref.1, f32[8,128]{1,0:T(8,128)} %potential_ref.1), custom_call_target="tpu_custom_call" | custom-call | tf_op jit(solution)/shard_map/pack_levels_potential/pallas_call | solution.py:31
  2.0 8.0 %all-to-all-start = ((f32[16,16,128]{2,1,0:T(8,128)}), f32[16,16,128]{2,1,0:T(8,128)S(1)}, u32[]{:S(2)}, u32[]{:S(2)}) async-start(f32[16,16,128]{2,1,0:T(8,128)} %pack_levels_potential.1), calls=%async_computation | async-start | bytes 262144 | tf_op jit(solution)/shard_map/all_to_all | solution.py:514
  10.0 0.0 copy-start
  10.0 0.0 copy-start.1
  10.0 8.0 %regrid_product.1 = (bf16[6,128,1024]{2,1,0:T(8,128)(2,1)S(1)}, f32[6,64,1024]{2,1,0:T(8,128)S(1)}, f32[1,64,1024]{2,1,0:T(8,128)S(1)}, bf16[2,128,1024]{2,1,0:T...) custom-call(bf16[2,64,1024]{2,1,0:T(8,128)(2,1)} %conductivity_hbm.1, bf16[4,64,1024]{2,1,0:T(8,128)(2,1)} %wind_hbm.1, ...), custom_call_target="tpu_custom_call" | custom-call | flops 4294967296 | bytes 16777216 | tf_op jit(solution)/shard_map/regrid_product/pallas_call | solution.py:125
  18.1 0.0 all-to-all-done.gathered
  18.1 0.0 copy-done
  18.1 0.0 copy-done.1
  18.1 2.1 %level_integral.1 = (f32[16,24,128]{2,1,0:T(8,128)S(1)}, f32[32,128]{1,0:T(8,128)S(1)}) custom-call(s32[1,8]{1,0:T(1,128)S(1)} %copy-done, f32[64]{0:T(128)S(1)} %copy-done.1, f32[16,16,128]{2,1,0:T(8,128)S(1)} %all-to-all-done.gathered, bf16[6,128,1024]{2,1,0:T(8,128)(2,1)S(1)} %get-tuple-element.15.near_plain, ...), custom_call_target="tpu_custom_call" | custom-call | flops 4718592 | bytes 12582912 | tf_op jit(solution)/shard_map/level_integral/pallas_call | solution.py:239
  20.2 2.3 %collective-permute-start.1 = (f32[32,128]{1,0:T(8,128)S(1)}, f32[32,128]{1,0:T(8,128)S(1)}, u32[]{:S(2)}, u32[]{:S(2)}) collective-permute-start(f32[32,128]{1,0:T(8,128)S(1)} %get-tuple-element.24), channel_id=1, source_target_pairs={{0,7},{1,2},{2,1},{3,4},{4,3},{5,6},{6,5},{7,0},{8,15},{9,10},{10,... | collective-permute-start | bytes 49160 | tf_op jit(solution)/shard_map/ppermute | solution.py:500
  22.5 0.0 collective-permute-start
  22.5 2.1 %meridional_integral.1.merid = f32[16,8,128]{2,1,0:T(8,128)S(1)} custom-call(s32[1,8]{1,0:T(1,128)S(1)} %copy-done, f32[64]{0:T(128)S(1)} %copy-done.1, f32[16,16,128]{2,1,0:T(8,128)S(1)} %all-to-all-done.gathered, f32[1,64,1024]{2,1,0:T(8,128)S(1)} %get-tuple-element.22.near, f32[7,64,1024]{2,1,0:T(8,128)} %get-tuple-element.23.far_hbm), custom_call_target="tpu_custom_call" | custom-call | flops 1835008 | bytes 3670016 | tf_op jit(solution)/shard_map/meridional_integral/pallas_call | solution.py:307
  24.6 0.0 collective-permute-done.1.across
  24.6 0.0 collective-permute-done.inside
  24.7 0.8 %assemble_sends.1 = bf16[16,64,128]{2,1,0:T(8,128)(2,1)} custom-call(f32[16,24,128]{2,1,0:T(8,128)S(1)} %get-tuple-element.19.combined, f32[16,8,128]{2,1,0:T(8,128)S(1)} %meridional_integral.1.merid, f32[32,128]{1,0:T(8,128)S(1)} %collective-permute-done.inside, f32[32,128]{1,0:T(8,128)S(1)} %collective-permute-done.1.across), custom_call_target="tpu_custom_call" | custom-call | tf_op jit(solution)/shard_map/assemble_sends/pallas_call | solution.py:373
  25.5 7.2 %all-to-all-start.1 = ((bf16[16,64,128]{2,1,0:T(8,128)(2,1)}), bf16[16,64,128]{2,1,0:T(8,128)(2,1)S(1)}, u32[]{:S(2)}, u32[]{:S(2)}) async-start(bf16[16,64,128]{2,1,0:T(8,128)(2,1)} %assemble_sends.1), calls=%async_computation.1 | async-start | bytes 524288 | tf_op jit(solution)/shard_map/all_to_all | solution.py:525
  32.7 7.5 %electric_to_geo.1 = f32[2,1024]{1,0:T(2,128)} custom-call(s32[1,8]{1,0:T(1,128)S(1)} %copy-done, f32[16,16,128]{2,1,0:T(8,128)S(1)} %all-to-all-done.gathered, f32[32,128]{1,0:T(8,128)S(1)} %collective-permute-done.inside, f32[32,128]{1,0:T(8,128)S(1)} %collective-permute-done.1.across, bf16[8,1024,1024]{2,1,0:T(8,128)(2,1)} %tiles_hbm.3), custom_call_target="tpu_custom_call" | custom-call | flops 134217728 | bytes 16777216 | tf_op jit(solution)/shard_map/electric_to_geo/pallas_call | solution.py:424
  40.2 1.5 %all-to-all-done.1.received = bf16[16,64,128]{2,1,0:T(8,128)(2,1)S(1)} async-done(((bf16[16,64,128]{2,1,0:T(8,128)(2,1)}), bf16[16,64,128]{2,1,0:T(8,128)(2,1)S(1)}, u32[]{:S(2)}, u32[]{:S(2)}) %all-to-all-start.1) | async-done | bytes 262176 | tf_op jit(solution)/shard_map/all_to_all | solution.py:525
  41.8 0.7 %stencil_source.1 = (f32[9,8,128]{2,1,0:T(8,128)}, f32[8,128]{1,0:T(8,128)}) custom-call(bf16[16,64,128]{2,1,0:T(8,128)(2,1)S(1)} %all-to-all-done.1.received), custom_call_target="tpu_custom_call" | custom-call | tf_op jit(solution)/shard_map/stencil_source/pallas_call | solution.py:483
Async XLA Ops:
  2.0 16.1 %all-to-all-start = ((f32[16,16,128]{2,1,0:T(8,128)}), f32[16,16,128]{2,1,0:T(8,128)S(1)}, u32[]{:S(2)}, u32[]{:S(2)}) async-start(f32[16,16,128]{2,1,0:T(8,128)} %pack_levels_potential.1), calls=%async_computation | async-start | bytes 262144 | tf_op jit(solution)/shard_map/all_to_all | solution.py:514
  10.0 8.1 %copy-start = (s32[1,8]{1,0:T(1,128)S(1)}, s32[1,8]{1,0:T(1,128)}, u32[]{:S(2)}) copy-start(s32[1,8]{1,0:T(1,128)} %targets.5) | copy-start | bytes 100
  10.0 8.1 %copy-start.1 = (f32[64]{0:T(128)S(1)}, f32[64]{0:T(128)}, u32[]{:S(2)}) copy-start(f32[64]{0:T(128)} %level_weights.3) | copy-start | bytes 772
  20.2 4.5 %collective-permute-start.1 = (f32[32,128]{1,0:T(8,128)S(1)}, f32[32,128]{1,0:T(8,128)S(1)}, u32[]{:S(2)}, u32[]{:S(2)}) collective-permute-start(f32[32,128]{1,0:T(8,128)S(1)} %get-tuple-element.24), channel_id=1, source_target_pairs={{0,7},{1,2},{2,1},{3,4},{4,3},{5,6},{6,5},{7,0},{8,15},{9,10},{10,... | collective-permute-start | bytes 49160 | tf_op jit(solution)/shard_map/ppermute | solution.py:500
  22.5 2.2 %collective-permute-start = (f32[32,128]{1,0:T(8,128)S(1)}, f32[32,128]{1,0:T(8,128)S(1)}, u32[]{:S(2)}, u32[]{:S(2)}) collective-permute-start(f32[32,128]{1,0:T(8,128)S(1)} %get-tuple-element.24), channel_id=1, source_target_pairs={{0,1},{1,0},{2,3},{3,2},{4,5},{5,4},{6,7},{7,6},{8,9},{9,8},{10,11... | collective-permute-start | bytes 49160 | tf_op jit(solution)/shard_map/ppermute | solution.py:500
  25.5 16.3 %all-to-all-start.1 = ((bf16[16,64,128]{2,1,0:T(8,128)(2,1)}), bf16[16,64,128]{2,1,0:T(8,128)(2,1)S(1)}, u32[]{:S(2)}, u32[]{:S(2)}) async-start(bf16[16,64,128]{2,1,0:T(8,128)(2,1)} %assemble_sends.1), calls=%async_computation.1 | async-start | bytes 524288 | tf_op jit(solution)/shard_map/all_to_all | solution.py:525

commit v6 on v5

--- a/solution.py
+++ b/solution.py
@@ -14,6 +14,7 @@
 SMALL = 8 * 2**20
 CHUNK = 2 * COLS
 FAR_TILES = 2
+ORDER = [5, 6, 9, 10, 1, 2, 4, 7, 8, 11, 13, 14, 0, 3, 12, 15]
 VMEM_SPEC = pl.BlockSpec(memory_space=pltpu.VMEM)
 HBM_SPEC = pl.BlockSpec(memory_space=pltpu.HBM)
 SMEM_SPEC = pl.BlockSpec(memory_space=pltpu.SMEM)
@@ -356,7 +357,7 @@
             columns = jnp.where((lanes >= 2 * f) & (lanes < 2 * f + 2), moved, columns)
 
         def put(start, *blocks):
-            out_ref[b, start : start + 2 * ROWS, :] = jnp.concatenate(blocks, 0).astype(jnp.bfloat16)
+            out_ref[ORDER.index(b), start : start + 2 * ROWS, :] = jnp.concatenate(blocks, 0).astype(jnp.bfloat16)
 
         put(0, combined[b, 0:8], combined[b, 8:16])
         put(16, *both_parts(combined[b, 16:24]))
@@ -522,7 +523,7 @@
     inside, across = lon_neighbours(edges)
     merid = meridional(tile_targets, level_weights, gathered, near_merid, far_merid)
     sends = assemble(combined, merid, inside, across)
-    received = lax.all_to_all(sends, "lat", 0, 0, tiled=True)
+    received = lax.all_to_all(sends, "lat", 0, 0, axis_index_groups=[ORDER], tiled=True)
     geo_field = backward(tile_targets, gathered, inside, across, tiles)
     stencil, source_term = stencil_source(received)
     return stencil, source_term, geo_field

time: 42.9 us -> 42.4 us (0.988)
  waiting for transfers between devices: 1.56 us -> 0.54 us
  starting transfers between devices: 17.4 us -> 17.9 us
    all_to_all x1, waiting for transfers between devices: 1.51 us -> 0.5 us  [per_device(): lax.all_to_all(sends, 'lat', 0, 0, axis_index_groups=[ORDER], tiled=True)]
    all_to_all x1, starting transfers between devices: 7.22 us -> 7.7 us  [per_device(): lax.all_to_all(sends, 'lat', 0, 0, axis_index_groups=[ORDER], tiled=True)]
where the time goes in v6:
time: 42.4 us; the launch traced here: 41.9 us
  Pallas kernels  22.7 us (54%)
  starting transfers between devices  17.9 us (42%)
  between operations  0.71 us (2%)
  waiting for transfers between devices  0.54 us (1%)
    pallas_call x1, Pallas kernels, product(): pl.pallas_call(product_kernel, out_shape=(pltpu.VMEM(*plain(near_count)),...  8.05 us
    all_to_all x1, starting transfers between devices, per_device(): gathered = lax.all_to_all(packed, 'lat', 0, 0, tiled=True)  7.96 us
    all_to_all x1, starting transfers between devices, per_device(): lax.all_to_all(sends, 'lat', 0, 0, axis_index_groups=[ORDER], tiled=True)  7.7 us
    pallas_call x1, Pallas kernels, backward(): pl.pallas_call(backward_kernel, out_shape=jax.ShapeDtypeStruct((2, geo_ce...  7.52 us
    ppermute x1, starting transfers between devices, lon_neighbours(): lax.ppermute(block, 'lon', across)  2.26 us
    pallas_call x1, Pallas kernels, meridional(): pl.pallas_call(meridional_kernel, out_shape=pltpu.VMEM((n_lat, ROWS, COLS...  2.14 us
    pallas_call x1, Pallas kernels, integral(): pl.pallas_call(integral_kernel, out_shape=(pltpu.VMEM((n_lat, 3 * ROWS, C...  2.11 us
    pallas_call x1, Pallas kernels, pack(): pl.pallas_call(pack_kernel, out_shape=pltpu.VMEM((n_lat, 2 * ROWS, COLS),...  1.37 us
  transfers between devices with their start and end apart: 4, of which 1 were waited for; matrix products, arithmetic and copies ran while one was open for 0% of the time, Pallas kernels for 42%

profile of v6, /device:TPU:0, one launch (start us, length us, event | category | flops | bytes accessed | tf_op | source)
XLA Modules:
  0.0 41.9 jit_solution(17316008122836882420)
XLA Ops:
  0.6 1.4 %pack_levels_potential.1 = f32[16,16,128]{2,1,0:T(8,128)} custom-call(s32[2,8,128]{2,1,0:T(8,128)} %levels_ref.1, f32[8,128]{1,0:T(8,128)} %potential_ref.1), custom_call_target="tpu_custom_call" | custom-call | tf_op jit(solution)/shard_map/pack_levels_potential/pallas_call | solution.py:32
  2.0 8.0 %all-to-all-start = ((f32[16,16,128]{2,1,0:T(8,128)}), f32[16,16,128]{2,1,0:T(8,128)S(1)}, u32[]{:S(2)}, u32[]{:S(2)}) async-start(f32[16,16,128]{2,1,0:T(8,128)} %pack_levels_potential.1), calls=%async_computation | async-start | bytes 262144 | tf_op jit(solution)/shard_map/all_to_all | solution.py:515
  10.0 0.0 copy-start
  10.0 0.0 copy-start.1
  10.0 8.0 %regrid_product.1 = (bf16[6,128,1024]{2,1,0:T(8,128)(2,1)S(1)}, f32[6,64,1024]{2,1,0:T(8,128)S(1)}, f32[1,64,1024]{2,1,0:T(8,128)S(1)}, bf16[2,128,1024]{2,1,0:T...) custom-call(bf16[2,64,1024]{2,1,0:T(8,128)(2,1)} %conductivity_hbm.1, bf16[4,64,1024]{2,1,0:T(8,128)(2,1)} %wind_hbm.1, ...), custom_call_target="tpu_custom_call" | custom-call | flops 4294967296 | bytes 16777216 | tf_op jit(solution)/shard_map/regrid_product/pallas_call | solution.py:126
  18.1 0.0 all-to-all-done.gathered
  18.1 0.0 copy-done
  18.1 0.0 copy-done.1
  18.1 2.1 %level_integral.1 = (f32[16,24,128]{2,1,0:T(8,128)S(1)}, f32[32,128]{1,0:T(8,128)S(1)}) custom-call(s32[1,8]{1,0:T(1,128)S(1)} %copy-done, f32[64]{0:T(128)S(1)} %copy-done.1, f32[16,16,128]{2,1,0:T(8,128)S(1)} %all-to-all-done.gathered, bf16[6,128,1024]{2,1,0:T(8,128)(2,1)S(1)} %get-tuple-element.15.near_plain, ...), custom_call_target="tpu_custom_call" | custom-call | flops 4718592 | bytes 12582912 | tf_op jit(solution)/shard_map/level_integral/pallas_call | solution.py:240
  20.2 2.3 %collective-permute-start.1 = (f32[32,128]{1,0:T(8,128)S(1)}, f32[32,128]{1,0:T(8,128)S(1)}, u32[]{:S(2)}, u32[]{:S(2)}) collective-permute-start(f32[32,128]{1,0:T(8,128)S(1)} %get-tuple-element.24), channel_id=1, source_target_pairs={{0,7},{1,2},{2,1},{3,4},{4,3},{5,6},{6,5},{7,0},{8,15},{9,10},{10,... | collective-permute-start | bytes 49160 | tf_op jit(solution)/shard_map/ppermute | solution.py:501
  22.5 0.0 collective-permute-start
  22.5 2.1 %meridional_integral.1.merid = f32[16,8,128]{2,1,0:T(8,128)S(1)} custom-call(s32[1,8]{1,0:T(1,128)S(1)} %copy-done, f32[64]{0:T(128)S(1)} %copy-done.1, f32[16,16,128]{2,1,0:T(8,128)S(1)} %all-to-all-done.gathered, f32[1,64,1024]{2,1,0:T(8,128)S(1)} %get-tuple-element.22.near, f32[7,64,1024]{2,1,0:T(8,128)} %get-tuple-element.23.far_hbm), custom_call_target="tpu_custom_call" | custom-call | flops 1835008 | bytes 3670016 | tf_op jit(solution)/shard_map/meridional_integral/pallas_call | solution.py:308
  24.6 0.0 collective-permute-done.1.across
  24.6 0.0 collective-permute-done.inside
  24.7 0.8 %assemble_sends.1 = bf16[16,64,128]{2,1,0:T(8,128)(2,1)} custom-call(f32[16,24,128]{2,1,0:T(8,128)S(1)} %get-tuple-element.19.combined, f32[16,8,128]{2,1,0:T(8,128)S(1)} %meridional_integral.1.merid, f32[32,128]{1,0:T(8,128)S(1)} %collective-permute-done.inside, f32[32,128]{1,0:T(8,128)S(1)} %collective-permute-done.1.across), custom_call_target="tpu_custom_call" | custom-call | tf_op jit(solution)/shard_map/assemble_sends/pallas_call | solution.py:374
  25.5 7.7 %all-to-all-start.1 = ((bf16[16,64,128]{2,1,0:T(8,128)(2,1)}), bf16[16,64,128]{2,1,0:T(8,128)(2,1)S(1)}, u32[]{:S(2)}, u32[]{:S(2)}) async-start(bf16[16,64,128]{2,1,0:T(8,128)(2,1)} %assemble_sends.1), calls=%async_computation.1 | async-start | bytes 524288 | tf_op jit(solution)/shard_map/all_to_all | solution.py:526
  33.2 7.5 %electric_to_geo.1 = f32[2,1024]{1,0:T(2,128)} custom-call(s32[1,8]{1,0:T(1,128)S(1)} %copy-done, f32[16,16,128]{2,1,0:T(8,128)S(1)} %all-to-all-done.gathered, f32[32,128]{1,0:T(8,128)S(1)} %collective-permute-done.inside, f32[32,128]{1,0:T(8,128)S(1)} %collective-permute-done.1.across, bf16[8,1024,1024]{2,1,0:T(8,128)(2,1)} %tiles_hbm.3), custom_call_target="tpu_custom_call" | custom-call | flops 134217728 | bytes 16777216 | tf_op jit(solution)/shard_map/electric_to_geo/pallas_call | solution.py:425
  40.7 0.5 %all-to-all-done.1.received = bf16[16,64,128]{2,1,0:T(8,128)(2,1)S(1)} async-done(((bf16[16,64,128]{2,1,0:T(8,128)(2,1)}), bf16[16,64,128]{2,1,0:T(8,128)(2,1)S(1)}, u32[]{:S(2)}, u32[]{:S(2)}) %all-to-all-start.1) | async-done | bytes 262176 | tf_op jit(solution)/shard_map/all_to_all | solution.py:526
  41.2 0.7 %stencil_source.1 = (f32[9,8,128]{2,1,0:T(8,128)}, f32[8,128]{1,0:T(8,128)}) custom-call(bf16[16,64,128]{2,1,0:T(8,128)(2,1)S(1)} %all-to-all-done.1.received), custom_call_target="tpu_custom_call" | custom-call | tf_op jit(solution)/shard_map/stencil_source/pallas_call | solution.py:484
Async XLA Ops:
  2.0 16.1 %all-to-all-start = ((f32[16,16,128]{2,1,0:T(8,128)}), f32[16,16,128]{2,1,0:T(8,128)S(1)}, u32[]{:S(2)}, u32[]{:S(2)}) async-start(f32[16,16,128]{2,1,0:T(8,128)} %pack_levels_potential.1), calls=%async_computation | async-start | bytes 262144 | tf_op jit(solution)/shard_map/all_to_all | solution.py:515
  10.0 8.1 %copy-start = (s32[1,8]{1,0:T(1,128)S(1)}, s32[1,8]{1,0:T(1,128)}, u32[]{:S(2)}) copy-start(s32[1,8]{1,0:T(1,128)} %targets.5) | copy-start | bytes 100
  10.0 8.1 %copy-start.1 = (f32[64]{0:T(128)S(1)}, f32[64]{0:T(128)}, u32[]{:S(2)}) copy-start(f32[64]{0:T(128)} %level_weights.3) | copy-start | bytes 772
  20.2 4.5 %collective-permute-start.1 = (f32[32,128]{1,0:T(8,128)S(1)}, f32[32,128]{1,0:T(8,128)S(1)}, u32[]{:S(2)}, u32[]{:S(2)}) collective-permute-start(f32[32,128]{1,0:T(8,128)S(1)} %get-tuple-element.24), channel_id=1, source_target_pairs={{0,7},{1,2},{2,1},{3,4},{4,3},{5,6},{6,5},{7,0},{8,15},{9,10},{10,... | collective-permute-start | bytes 49160 | tf_op jit(solution)/shard_map/ppermute | solution.py:501
  22.5 2.2 %collective-permute-start = (f32[32,128]{1,0:T(8,128)S(1)}, f32[32,128]{1,0:T(8,128)S(1)}, u32[]{:S(2)}, u32[]{:S(2)}) collective-permute-start(f32[32,128]{1,0:T(8,128)S(1)} %get-tuple-element.24), channel_id=1, source_target_pairs={{0,1},{1,0},{2,3},{3,2},{4,5},{5,4},{6,7},{7,6},{8,9},{9,8},{10,11... | collective-permute-start | bytes 49160 | tf_op jit(solution)/shard_map/ppermute | solution.py:501
  25.5 15.7 %all-to-all-start.1 = ((bf16[16,64,128]{2,1,0:T(8,128)(2,1)}), bf16[16,64,128]{2,1,0:T(8,128)(2,1)S(1)}, u32[]{:S(2)}, u32[]{:S(2)}) async-start(bf16[16,64,128]{2,1,0:T(8,128)(2,1)} %assemble_sends.1), calls=%async_computation.1 | async-start | bytes 524288 | tf_op jit(solution)/shard_map/all_to_all | solution.py:526

commit v7 on v6

--- a/solution.py
+++ b/solution.py
@@ -170,7 +170,7 @@
 
 
 def integral_kernel(
-    targets, level_weights, gathered, near_plain, near_zonal, far_plain_hbm, far_zonal_hbm, combined, edges,
+    targets, level_weights, gathered, near_plain, near_zonal, far_plain_hbm, far_zonal_hbm, far_merid_hbm, combined, edges, far_merid,
     weights, plain, mirrored, far_plain, far_zonal, sems,
 ):
     near_count, far_count = near_plain.shape[0], far_plain.shape[0]
@@ -186,6 +186,12 @@
     for i in range(far_count):
         for copy in far_inputs(i):
             copy.start()
+    rest = [
+        pltpu.make_async_copy(far_merid_hbm.at[i], far_merid.at[i], sems.at[2 * far_count + i])
+        for i in range(far_merid.shape[0])
+    ]
+    for copy in rest:
+        copy.start()
     fill_weights(level_weights, weights)
     plain[...] = jnp.zeros_like(plain)
     mirrored[...] = jnp.zeros_like(mirrored)
@@ -231,9 +237,11 @@
         rows = slice(f * ROWS, (f + 1) * ROWS)
         edges[rows, :] = both_edges(lambda b: combined[b, rows, :])
     edges[3 * ROWS : 4 * ROWS, :] = both_edges(lambda b: gathered[b, ROWS : 2 * ROWS, :])
-
-
-def integral(targets, level_weights, gathered, near, far):
+    for copy in rest:
+        copy.wait()
+
+
+def integral(targets, level_weights, gathered, near, far, far_merid):
     far_count = far[0].shape[0]
     levels_n = level_weights.shape[0]
     n_lat = gathered.shape[0]
@@ -242,27 +250,28 @@
         out_shape=(
             pltpu.VMEM((n_lat, 3 * ROWS, COLS), jnp.float32),
             pltpu.VMEM((4 * ROWS, COLS), jnp.float32),
-        ),
-        in_specs=[SMEM_SPEC] * 2 + [VMEM_SPEC] * 3 + [HBM_SPEC] * 2,
-        out_specs=(VMEM_SPEC, VMEM_SPEC),
+            pltpu.VMEM(far_merid.shape, far_merid.dtype),
+        ),
+        in_specs=[SMEM_SPEC] * 2 + [VMEM_SPEC] * 3 + [HBM_SPEC] * 3,
+        out_specs=(VMEM_SPEC,) * 3,
         scratch_shapes=[
             pltpu.VMEM((levels_n, COLS), jnp.float32),
             pltpu.VMEM((n_lat, 3 * ROWS, COLS), jnp.float32),
             pltpu.VMEM((n_lat, 3 * ROWS, COLS), jnp.float32),
             pltpu.VMEM(far[0].shape, far[0].dtype),
             pltpu.VMEM(far[1].shape, far[1].dtype),
-            pltpu.SemaphoreType.DMA((2 * far_count,)),
+            pltpu.SemaphoreType.DMA((2 * far_count + far_merid.shape[0],)),
         ],
         compiler_params=pltpu.CompilerParams(vmem_limit_bytes=SCOPED),
         cost_estimate=pl.CostEstimate(
             flops=6 * near[0].size, bytes_accessed=16 * near[0].size, transcendentals=0
         ),
         name="level_integral",
-    )(in_smem(targets), in_smem(level_weights), in_vmem(gathered), *map(in_vmem, near), *map(in_hbm, far))
+    )(in_smem(targets), in_smem(level_weights), in_vmem(gathered), *map(in_vmem, near), *map(in_hbm, far), in_hbm(far_merid))
 
 
 def meridional_kernel(
-    targets, level_weights, gathered, near, far_hbm, out_ref, weights, total, far, sems
+    targets, level_weights, gathered, near, far, out_ref, weights, total
 ):
     far_count = far.shape[0]
     tile_count = targets.shape[1]
@@ -270,11 +279,6 @@
     n_lat = gathered.shape[0]
     shift = tile_count - FAR_TILES
 
-    def far_input(i):
-        return pltpu.make_async_copy(far_hbm.at[i], far.at[i], sems.at[i])
-
-    for i in range(far_count):
-        far_input(i).start()
     fill_weights(level_weights, weights)
     total[...] = jnp.zeros_like(total)
 
@@ -291,7 +295,6 @@
 
     @pl.loop(0, far_count)
     def _(i):
-        far_input(i).wait()
         integrate(i, far, i)
 
     merid = [total[0, b] + total[1, b] for b in range(n_lat)]
@@ -308,20 +311,18 @@
     return pl.pallas_call(
         meridional_kernel,
         out_shape=pltpu.VMEM((n_lat, ROWS, COLS), jnp.float32),
-        in_specs=[SMEM_SPEC] * 2 + [VMEM_SPEC] * 2 + [HBM_SPEC],
+        in_specs=[SMEM_SPEC] * 2 + [VMEM_SPEC] * 3,
         out_specs=VMEM_SPEC,
         scratch_shapes=[
             pltpu.VMEM((levels_n, COLS), jnp.float32),
             pltpu.VMEM((2, n_lat, ROWS, COLS), jnp.float32),
-            pltpu.VMEM(far.shape, far.dtype),
-            pltpu.SemaphoreType.DMA((far.shape[0],)),
         ],
-        compiler_params=pltpu.CompilerParams(vmem_limit_bytes=SCOPED),
+        compiler_params=pltpu.CompilerParams(vmem_limit_bytes=SMALL),
         cost_estimate=pl.CostEstimate(
             flops=4 * far.size, bytes_accessed=8 * far.size, transcendentals=0
         ),
         name="meridional_integral",
-    )(in_smem(targets), in_smem(level_weights), in_vmem(gathered), in_vmem(near), in_hbm(far))
+    )(in_smem(targets), in_smem(level_weights), in_vmem(gathered), in_vmem(near), in_vmem(far))
 
 
 def assemble_kernel(combined, merid, inside, across, out_ref):
@@ -516,8 +517,8 @@
     near_plain, near_zonal, near_merid, far_plain, far_zonal, far_merid = product(
         in_hbm(conductivity), in_hbm(wind_terms), tiles, tiles.shape[0] - FAR_TILES
     )
-    combined, edges = integral(
-        tile_targets, level_weights, gathered, (near_plain, near_zonal), (far_plain, far_zonal)
+    combined, edges, far_merid = integral(
+        tile_targets, level_weights, gathered, (near_plain, near_zonal), (far_plain, far_zonal), far_merid
     )
     edges, near_merid = lax.optimization_barrier((edges, near_merid))
     inside, across = lon_neighbours(edges)

time: 42.4 us -> 42.3 us (level)
  Pallas kernels: 22.7 us -> 22.1 us
  waiting for transfers between devices: 0.54 us -> 1.1 us
    ppermute x1, waiting for transfers between devices: 0.04 us -> 0.95 us  [lon_neighbours(): lax.ppermute(block, 'lon', across)]
    pallas_call x1, Pallas kernels: 2.14 us -> 1.23 us  [meridional(): pl.pallas_call(meridional_kernel, out_shape=pltpu.VMEM((n_lat, ROWS, COLS...]
  transfers between devices with their start and end apart: 4 -> 4, of which waited for: 1 -> 2; matrix products, arithmetic and copies ran while one was open for 0% -> 0% of each run, Pallas kernels for 42% -> 40%
where the time goes in v7:
time: 42.3 us; the launch traced here: 41.9 us
  Pallas kernels  22.1 us (52%)
  starting transfers between devices  17.9 us (42%)
  waiting for transfers between devices  1.1 us (3%)
  between operations  0.71 us (2%)
    pallas_call x1, Pallas kernels, product(): pl.pallas_call(product_kernel, out_shape=(pltpu.VMEM(*plain(near_count)),...  8.05 us
    all_to_all x1, starting transfers between devices, per_device(): gathered = lax.all_to_all(packed, 'lat', 0, 0, tiled=True)  7.96 us
    all_to_all x1, starting transfers between devices, per_device(): lax.all_to_all(sends, 'lat', 0, 0, axis_index_groups=[ORDER], tiled=True)  7.7 us
    pallas_call x1, Pallas kernels, backward(): pl.pallas_call(backward_kernel, out_shape=jax.ShapeDtypeStruct((2, geo_ce...  7.52 us
    pallas_call x1, Pallas kernels, integral(): pl.pallas_call(integral_kernel, out_shape=(pltpu.VMEM((n_lat, 3 * ROWS, C...  2.38 us
    ppermute x1, starting transfers between devices, lon_neighbours(): lax.ppermute(block, 'lon', across)  2.26 us
    pallas_call x1, Pallas kernels, pack(): pl.pallas_call(pack_kernel, out_shape=pltpu.VMEM((n_lat, 2 * ROWS, COLS),...  1.37 us
    pallas_call x1, Pallas kernels, meridional(): pl.pallas_call(meridional_kernel, out_shape=pltpu.VMEM((n_lat, ROWS, COLS...  1.23 us
  transfers between devices with their start and end apart: 4, of which 2 were waited for; matrix products, arithmetic and copies ran while one was open for 0% of the time, Pallas kernels for 40%

profile of v7, /device:TPU:0, one launch (start us, length us, event | category | flops | bytes accessed | tf_op | source)
XLA Modules:
  0.0 41.9 jit_solution(16265724934958078944)
XLA Ops:
  0.6 1.4 %pack_levels_potential.1 = f32[16,16,128]{2,1,0:T(8,128)} custom-call(s32[2,8,128]{2,1,0:T(8,128)} %levels_ref.1, f32[8,128]{1,0:T(8,128)} %potential_ref.1), custom_call_target="tpu_custom_call" | custom-call | tf_op jit(solution)/shard_map/pack_levels_potential/pallas_call | solution.py:32
  2.0 8.0 %all-to-all-start = ((f32[16,16,128]{2,1,0:T(8,128)}), f32[16,16,128]{2,1,0:T(8,128)S(1)}, u32[]{:S(2)}, u32[]{:S(2)}) async-start(f32[16,16,128]{2,1,0:T(8,128)} %pack_levels_potential.1), calls=%async_computation | async-start | bytes 262144 | tf_op jit(solution)/shard_map/all_to_all | solution.py:516
  10.0 0.0 copy-start
  10.0 0.0 copy-start.1
  10.0 8.0 %regrid_product.1 = (bf16[6,128,1024]{2,1,0:T(8,128)(2,1)S(1)}, f32[6,64,1024]{2,1,0:T(8,128)S(1)}, f32[1,64,1024]{2,1,0:T(8,128)S(1)}, bf16[2,128,1024]{2,1,0:T...) custom-call(bf16[2,64,1024]{2,1,0:T(8,128)(2,1)} %conductivity_hbm.1, bf16[4,64,1024]{2,1,0:T(8,128)(2,1)} %wind_hbm.1, ...), custom_call_target="tpu_custom_call" | custom-call | flops 4294967296 | bytes 16777216 | tf_op jit(solution)/shard_map/regrid_product/pallas_call | solution.py:126
  18.1 0.0 all-to-all-done.gathered
  18.1 0.0 copy-done
  18.1 0.0 copy-done.1
  18.1 2.4 %level_integral.1 = (f32[16,24,128]{2,1,0:T(8,128)S(1)}, f32[32,128]{1,0:T(8,128)S(1)}, f32[7,64,1024]{2,1,0:T(8,128)S(1)}) custom-call(s32[1,8]{1,0:T(1,128)S(1)} %copy-done, f32[64]{0:T(128)S(1)} %copy-done.1, f32[16,16,128]{2,1,0:T(8,128)S(1)} %all-to-all-done.gathered, bf16[6,128,1024]{2,1,0:T(8,128)(2,1)S(1)} %get-tuple-element.16.near_plain, ...), custom_call_target="tpu_custom_call" | custom-call | flops 4718592 | bytes 12582912 | tf_op jit(solution)/shard_map/level_integral/pallas_call | solution.py:248
  20.5 2.3 %collective-permute-start.1 = (f32[32,128]{1,0:T(8,128)S(1)}, f32[32,128]{1,0:T(8,128)S(1)}, u32[]{:S(2)}, u32[]{:S(2)}) collective-permute-start(f32[32,128]{1,0:T(8,128)S(1)} %get-tuple-element.26), channel_id=1, source_target_pairs={{0,7},{1,2},{2,1},{3,4},{4,3},{5,6},{6,5},{7,0},{8,15},{9,10},{10,... | collective-permute-start | bytes 49160 | tf_op jit(solution)/shard_map/ppermute | solution.py:502
  22.7 0.0 collective-permute-start
  22.7 1.2 %meridional_integral.1.merid = f32[16,8,128]{2,1,0:T(8,128)S(1)} custom-call(s32[1,8]{1,0:T(1,128)S(1)} %copy-done, f32[64]{0:T(128)S(1)} %copy-done.1, f32[16,16,128]{2,1,0:T(8,128)S(1)} %all-to-all-done.gathered, f32[1,64,1024]{2,1,0:T(8,128)S(1)} %get-tuple-element.24.near, f32[7,64,1024]{2,1,0:T(8,128)S(1)} %get-tuple-element.25.far), custom_call_target="tpu_custom_call" | custom-call | flops 1835008 | bytes 3670016 | tf_op jit(solution)/shard_map/meridional_integral/pallas_call | solution.py:311
  24.0 1.0 %collective-permute-done.1.across = f32[32,128]{1,0:T(8,128)S(1)} collective-permute-done((f32[32,128]{1,0:T(8,128)S(1)}, f32[32,128]{1,0:T(8,128)S(1)}, u32[]{:S(2)}, u32[]{:S(2)}) %collective-permute-start.1) | collective-permute-done | bytes 16416 | tf_op jit(solution)/shard_map/ppermute | solution.py:502
  24.9 0.0 collective-permute-done.inside
  24.9 0.8 %assemble_sends.1 = bf16[16,64,128]{2,1,0:T(8,128)(2,1)} custom-call(f32[16,24,128]{2,1,0:T(8,128)S(1)} %get-tuple-element.21.combined, f32[16,8,128]{2,1,0:T(8,128)S(1)} %meridional_integral.1.merid, f32[32,128]{1,0:T(8,128)S(1)} %collective-permute-done.inside, f32[32,128]{1,0:T(8,128)S(1)} %collective-permute-done.1.across), custom_call_target="tpu_custom_call" | custom-call | tf_op jit(solution)/shard_map/assemble_sends/pallas_call | solution.py:375
  25.8 7.7 %all-to-all-start.1 = ((bf16[16,64,128]{2,1,0:T(8,128)(2,1)}), bf16[16,64,128]{2,1,0:T(8,128)(2,1)S(1)}, u32[]{:S(2)}, u32[]{:S(2)}) async-start(bf16[16,64,128]{2,1,0:T(8,128)(2,1)} %assemble_sends.1), calls=%async_computation.1 | async-start | bytes 524288 | tf_op jit(solution)/shard_map/all_to_all | solution.py:527
  33.5 7.5 %electric_to_geo.1 = f32[2,1024]{1,0:T(2,128)} custom-call(s32[1,8]{1,0:T(1,128)S(1)} %copy-done, f32[16,16,128]{2,1,0:T(8,128)S(1)} %all-to-all-done.gathered, f32[32,128]{1,0:T(8,128)S(1)} %collective-permute-done.inside, f32[32,128]{1,0:T(8,128)S(1)} %collective-permute-done.1.across, bf16[8,1024,1024]{2,1,0:T(8,128)(2,1)} %tiles_hbm.3), custom_call_target="tpu_custom_call" | custom-call | flops 134217728 | bytes 16777216 | tf_op jit(solution)/shard_map/electric_to_geo/pallas_call | solution.py:426
  41.0 0.1 all-to-all-done.1.received
  41.1 0.7 %stencil_source.1 = (f32[9,8,128]{2,1,0:T(8,128)}, f32[8,128]{1,0:T(8,128)}) custom-call(bf16[16,64,128]{2,1,0:T(8,128)(2,1)S(1)} %all-to-all-done.1.received), custom_call_target="tpu_custom_call" | custom-call | tf_op jit(solution)/shard_map/stencil_source/pallas_call | solution.py:485
Async XLA Ops:
  2.0 16.1 %all-to-all-start = ((f32[16,16,128]{2,1,0:T(8,128)}), f32[16,16,128]{2,1,0:T(8,128)S(1)}, u32[]{:S(2)}, u32[]{:S(2)}) async-start(f32[16,16,128]{2,1,0:T(8,128)} %pack_levels_potential.1), calls=%async_computation | async-start | bytes 262144 | tf_op jit(solution)/shard_map/all_to_all | solution.py:516
  10.0 8.1 %copy-start = (s32[1,8]{1,0:T(1,128)S(1)}, s32[1,8]{1,0:T(1,128)}, u32[]{:S(2)}) copy-start(s32[1,8]{1,0:T(1,128)} %targets.5) | copy-start | bytes 100
  10.0 8.1 %copy-start.1 = (f32[64]{0:T(128)S(1)}, f32[64]{0:T(128)}, u32[]{:S(2)}) copy-start(f32[64]{0:T(128)} %level_weights.3) | copy-start | bytes 772
  20.5 4.5 %collective-permute-start.1 = (f32[32,128]{1,0:T(8,128)S(1)}, f32[32,128]{1,0:T(8,128)S(1)}, u32[]{:S(2)}, u32[]{:S(2)}) collective-permute-start(f32[32,128]{1,0:T(8,128)S(1)} %get-tuple-element.26), channel_id=1, source_target_pairs={{0,7},{1,2},{2,1},{3,4},{4,3},{5,6},{6,5},{7,0},{8,15},{9,10},{10,... | collective-permute-start | bytes 49160 | tf_op jit(solution)/shard_map/ppermute | solution.py:502
  22.7 2.2 %collective-permute-start = (f32[32,128]{1,0:T(8,128)S(1)}, f32[32,128]{1,0:T(8,128)S(1)}, u32[]{:S(2)}, u32[]{:S(2)}) collective-permute-start(f32[32,128]{1,0:T(8,128)S(1)} %get-tuple-element.26), channel_id=1, source_target_pairs={{0,1},{1,0},{2,3},{3,2},{4,5},{5,4},{6,7},{7,6},{8,9},{9,8},{10,11... | collective-permute-start | bytes 49160 | tf_op jit(solution)/shard_map/ppermute | solution.py:502
  25.8 15.4 %all-to-all-start.1 = ((bf16[16,64,128]{2,1,0:T(8,128)(2,1)}), bf16[16,64,128]{2,1,0:T(8,128)(2,1)S(1)}, u32[]{:S(2)}, u32[]{:S(2)}) async-start(bf16[16,64,128]{2,1,0:T(8,128)(2,1)} %assemble_sends.1), calls=%async_computation.1 | async-start | bytes 524288 | tf_op jit(solution)/shard_map/all_to_all | solution.py:527

commit v8 on v7

--- a/solution.py
+++ b/solution.py
@@ -14,6 +14,8 @@
 SMALL = 8 * 2**20
 CHUNK = 2 * COLS
 FAR_TILES = 2
+HELD_TILES = 1
+HELD_PARTS = 8
 ORDER = [5, 6, 9, 10, 1, 2, 4, 7, 8, 11, 13, 14, 0, 3, 12, 15]
 VMEM_SPEC = pl.BlockSpec(memory_space=pltpu.VMEM)
 HBM_SPEC = pl.BlockSpec(memory_space=pltpu.HBM)
@@ -271,8 +273,18 @@
 
 
 def meridional_kernel(
-    targets, level_weights, gathered, near, far, out_ref, weights, total
+    targets, level_weights, gathered, near, far, tiles_hbm, out_ref, held, weights, total, sems
 ):
+    first = tiles_hbm.shape[0] - held.shape[0]
+    part = held.shape[1] // HELD_PARTS
+    hold = [
+        pltpu.make_async_copy(
+            tiles_hbm.at[first, pl.ds(i * part, part)], held.at[0, pl.ds(i * part, part)], sems.at[i]
+        )
+        for i in range(HELD_PARTS)
+    ]
+    for copy in hold:
+        copy.start()
     far_count = far.shape[0]
     tile_count = targets.shape[1]
     levels_n = level_weights.shape[0]
@@ -303,26 +315,32 @@
         below = merid[b - 1][ROWS - 1 : ROWS] if b > 0 else nothing
         above = merid[b + 1][0:1] if b + 1 < n_lat else nothing
         out_ref[b] = row_below(merid[b], below) - row_above(merid[b], above)
-
-
-def meridional(targets, level_weights, gathered, near, far):
+    for copy in hold:
+        copy.wait()
+
+
+def meridional(targets, level_weights, gathered, near, far, tiles):
     n_lat = gathered.shape[0]
     levels_n = level_weights.shape[0]
     return pl.pallas_call(
         meridional_kernel,
-        out_shape=pltpu.VMEM((n_lat, ROWS, COLS), jnp.float32),
-        in_specs=[SMEM_SPEC] * 2 + [VMEM_SPEC] * 3,
-        out_specs=VMEM_SPEC,
+        out_shape=(
+            pltpu.VMEM((n_lat, ROWS, COLS), jnp.float32),
+            pltpu.VMEM((HELD_TILES,) + tiles.shape[1:], tiles.dtype),
+        ),
+        in_specs=[SMEM_SPEC] * 2 + [VMEM_SPEC] * 3 + [HBM_SPEC],
+        out_specs=(VMEM_SPEC, VMEM_SPEC),
         scratch_shapes=[
             pltpu.VMEM((levels_n, COLS), jnp.float32),
             pltpu.VMEM((2, n_lat, ROWS, COLS), jnp.float32),
+            pltpu.SemaphoreType.DMA((HELD_PARTS,)),
         ],
         compiler_params=pltpu.CompilerParams(vmem_limit_bytes=SMALL),
         cost_estimate=pl.CostEstimate(
             flops=4 * far.size, bytes_accessed=8 * far.size, transcendentals=0
         ),
         name="meridional_integral",
-    )(in_smem(targets), in_smem(level_weights), in_vmem(gathered), in_vmem(near), in_vmem(far))
+    )(in_smem(targets), in_smem(level_weights), in_vmem(gathered), in_vmem(near), in_vmem(far), in_hbm(tiles))
 
 
 def assemble_kernel(combined, merid, inside, across, out_ref):
@@ -382,7 +400,7 @@
     )(in_vmem(combined), in_vmem(merid), in_vmem(inside), in_vmem(across))
 
 
-def backward_kernel(targets, gathered, inside, across, tiles_hbm, out_ref, zonal, merid, rows_ref, tiles, sems):
+def backward_kernel(targets, gathered, inside, across, held, tiles_hbm, out_ref, zonal, merid, rows_ref, tiles, sems):
     n_lat = gathered.shape[0]
     tile_count = tiles.shape[0]
     copies = [
@@ -405,13 +423,17 @@
         zonal[b] = -0.5 * (eastern - western)
         merid[b] = -0.5 * (row_above(here, above) - row_below(here, below))
     rows_ref[...] = jnp.zeros_like(rows_ref)
-    for k in range(tile_count):
+    for k in range(rows_ref.shape[0]):
         target = targets[0, k]
         for row in range(ROWS):
             columns = slice(row * COLS, (row + 1) * COLS)
             rows_ref[k, 0:1, columns] = zonal[target, row : row + 1, :]
             rows_ref[k, 1:2, columns] = merid[target, row : row + 1, :]
     total = jnp.zeros((ROWS, tiles.shape[2]), jnp.float32)
+    for i in range(held.shape[0]):
+        total += jnp.dot(
+            rows_ref[tile_count + i].astype(jnp.bfloat16), held[i], preferred_element_type=jnp.float32
+        )
     for k in range(tile_count):
         copies[k].wait()
         total += jnp.dot(
@@ -420,27 +442,27 @@
     out_ref[...] = total[0:2]
 
 
-def backward(targets, gathered, inside, across, tiles):
+def backward(targets, gathered, inside, across, held, tiles):
     n_lat = gathered.shape[0]
     tile_count, mag_cells, geo_cells = tiles.shape
     return pl.pallas_call(
         backward_kernel,
         out_shape=jax.ShapeDtypeStruct((2, geo_cells), jnp.float32),
-        in_specs=[SMEM_SPEC, VMEM_SPEC, VMEM_SPEC, VMEM_SPEC, HBM_SPEC],
+        in_specs=[SMEM_SPEC] + [VMEM_SPEC] * 4 + [HBM_SPEC],
         out_specs=VMEM_SPEC,
         scratch_shapes=[
             pltpu.VMEM((n_lat, ROWS, COLS), jnp.float32),
             pltpu.VMEM((n_lat, ROWS, COLS), jnp.float32),
             pltpu.VMEM((tile_count, ROWS, mag_cells), jnp.float32),
-            pltpu.VMEM(tiles.shape, tiles.dtype),
-            pltpu.SemaphoreType.DMA((tile_count,)),
+            pltpu.VMEM((tile_count - held.shape[0], mag_cells, geo_cells), tiles.dtype),
+            pltpu.SemaphoreType.DMA((tile_count - held.shape[0],)),
         ],
         compiler_params=pltpu.CompilerParams(vmem_limit_bytes=SCOPED),
         cost_estimate=pl.CostEstimate(
             flops=16 * tiles.size, bytes_accessed=2 * tiles.size, transcendentals=0
         ),
         name="electric_to_geo",
-    )(in_smem(targets), in_vmem(gathered), in_vmem(inside), in_vmem(across), tiles)
+    )(in_smem(targets), in_vmem(gathered), in_vmem(inside), in_vmem(across), in_vmem(held), tiles)
 
 
 def stencil_kernel(received, stencil_ref, source_ref):
@@ -522,10 +544,12 @@
     )
     edges, near_merid = lax.optimization_barrier((edges, near_merid))
     inside, across = lon_neighbours(edges)
-    merid = meridional(tile_targets, level_weights, gathered, near_merid, far_merid)
+    merid, held = meridional(
+        tile_targets, level_weights, gathered, near_merid, far_merid, tiles
+    )
     sends = assemble(combined, merid, inside, across)
     received = lax.all_to_all(sends, "lat", 0, 0, axis_index_groups=[ORDER], tiled=True)
-    geo_field = backward(tile_targets, gathered, inside, across, tiles)
+    geo_field = backward(tile_targets, gathered, inside, across, held, tiles)
     stencil, source_term = stencil_source(received)
     return stencil, source_term, geo_field
 

time: 42.3 us -> 42.6 us (level)
    all_to_all x1, waiting for transfers between devices: 0.14 us -> 1.07 us  [per_device(): lax.all_to_all(sends, 'lat', 0, 0, axis_index_groups=[ORDER], tiled=True)]
    pallas_call x1, Pallas kernels: 1.23 us -> 2.11 us  [meridional(): pl.pallas_call(meridional_kernel, out_shape=(pltpu.VMEM((n_lat, ROWS, COL...]
    ppermute x1, waiting for transfers between devices: 0.95 us -> 0.08 us  [lon_neighbours(): lax.ppermute(block, 'lon', across)]
    pallas_call x1, Pallas kernels: 7.52 us -> 6.92 us  [backward(): pl.pallas_call(backward_kernel, out_shape=jax.ShapeDtypeStruct((2, geo_ce...]
  transfers between devices with their start and end apart: 4 -> 4, of which waited for: 2 -> 2; matrix products, arithmetic and copies ran while one was open for 0% -> 0% of each run, Pallas kernels for 40% -> 41%
where the time goes in v8:
time: 42.6 us; the launch traced here: 42.2 us
  Pallas kernels  22.4 us (53%)
  starting transfers between devices  17.9 us (42%)
  waiting for transfers between devices  1.15 us (3%)
  between operations  0.71 us (2%)
    pallas_call x1, Pallas kernels, product(): pl.pallas_call(product_kernel, out_shape=(pltpu.VMEM(*plain(near_count)),...  8.05 us
    all_to_all x1, starting transfers between devices, per_device(): gathered = lax.all_to_all(packed, 'lat', 0, 0, tiled=True)  7.96 us
    all_to_all x1, starting transfers between devices, per_device(): lax.all_to_all(sends, 'lat', 0, 0, axis_index_groups=[ORDER], tiled=True)  7.69 us
    pallas_call x1, Pallas kernels, backward(): pl.pallas_call(backward_kernel, out_shape=jax.ShapeDtypeStruct((2, geo_ce...  6.92 us
    pallas_call x1, Pallas kernels, integral(): pl.pallas_call(integral_kernel, out_shape=(pltpu.VMEM((n_lat, 3 * ROWS, C...  2.38 us
    ppermute x1, starting transfers between devices, lon_neighbours(): lax.ppermute(block, 'lon', across)  2.25 us
    pallas_call x1, Pallas kernels, meridional(): pl.pallas_call(meridional_kernel, out_shape=(pltpu.VMEM((n_lat, ROWS, COL...  2.11 us
    pallas_call x1, Pallas kernels, pack(): pl.pallas_call(pack_kernel, out_shape=pltpu.VMEM((n_lat, 2 * ROWS, COLS),...  1.37 us
  transfers between devices with their start and end apart: 4, of which 2 were waited for; matrix products, arithmetic and copies ran while one was open for 0% of the time, Pallas kernels for 41%

profile of v8, /device:TPU:0, one launch (start us, length us, event | category | flops | bytes accessed | tf_op | source)
XLA Modules:
  0.0 42.2 jit_solution(15029207986613647025)
XLA Ops:
  0.6 1.4 %pack_levels_potential.1 = f32[16,16,128]{2,1,0:T(8,128)} custom-call(s32[2,8,128]{2,1,0:T(8,128)} %levels_ref.1, f32[8,128]{1,0:T(8,128)} %potential_ref.1), custom_call_target="tpu_custom_call" | custom-call | tf_op jit(solution)/shard_map/pack_levels_potential/pallas_call | solution.py:34
  2.0 8.0 %all-to-all-start = ((f32[16,16,128]{2,1,0:T(8,128)}), f32[16,16,128]{2,1,0:T(8,128)S(1)}, u32[]{:S(2)}, u32[]{:S(2)}) async-start(f32[16,16,128]{2,1,0:T(8,128)} %pack_levels_potential.1), calls=%async_computation | async-start | bytes 262144 | tf_op jit(solution)/shard_map/all_to_all | solution.py:538
  10.0 0.0 copy-start
  10.0 0.0 copy-start.1
  10.0 8.1 %regrid_product.1 = (bf16[6,128,1024]{2,1,0:T(8,128)(2,1)S(1)}, f32[6,64,1024]{2,1,0:T(8,128)S(1)}, f32[1,64,1024]{2,1,0:T(8,128)S(1)}, bf16[2,128,1024]{2,1,0:T...) custom-call(bf16[2,64,1024]{2,1,0:T(8,128)(2,1)} %conductivity_hbm.1, bf16[4,64,1024]{2,1,0:T(8,128)(2,1)} %wind_hbm.1, ...), custom_call_target="tpu_custom_call" | custom-call | flops 4294967296 | bytes 16777216 | tf_op jit(solution)/shard_map/regrid_product/pallas_call | solution.py:128
  18.1 0.0 all-to-all-done.gathered
  18.1 0.0 copy-done
  18.1 0.0 copy-done.1
  18.1 2.4 %level_integral.1 = (f32[16,24,128]{2,1,0:T(8,128)S(1)}, f32[32,128]{1,0:T(8,128)S(1)}, f32[7,64,1024]{2,1,0:T(8,128)S(1)}) custom-call(s32[1,8]{1,0:T(1,128)S(1)} %copy-done, f32[64]{0:T(128)S(1)} %copy-done.1, f32[16,16,128]{2,1,0:T(8,128)S(1)} %all-to-all-done.gathered, bf16[6,128,1024]{2,1,0:T(8,128)(2,1)S(1)} %get-tuple-element.18.near_plain, ...), custom_call_target="tpu_custom_call" | custom-call | flops 4718592 | bytes 12582912 | tf_op jit(solution)/shard_map/level_integral/pallas_call | solution.py:250
  20.5 2.3 %collective-permute-start.1 = (f32[32,128]{1,0:T(8,128)S(1)}, f32[32,128]{1,0:T(8,128)S(1)}, u32[]{:S(2)}, u32[]{:S(2)}) collective-permute-start(f32[32,128]{1,0:T(8,128)S(1)} %get-tuple-element.29), channel_id=1, source_target_pairs={{0,7},{1,2},{2,1},{3,4},{4,3},{5,6},{6,5},{7,0},{8,15},{9,10},{10,... | collective-permute-start | bytes 49160 | tf_op jit(solution)/shard_map/ppermute | solution.py:524
  22.7 0.0 collective-permute-start
  22.7 2.1 %meridional_integral.1 = (f32[16,8,128]{2,1,0:T(8,128)S(1)}, bf16[1,1024,1024]{2,1,0:T(8,128)(2,1)S(1)}) custom-call(s32[1,8]{1,0:T(1,128)S(1)} %copy-done, f32[64]{0:T(128)S(1)} %copy-done.1, f32[16,16,128]{2,1,0:T(8,128)S(1)} %all-to-all-done.gathered, f32[1,64,1024]{2,1,0:T(8,128)S(1)} %get-tuple-element.26.near, ...), custom_call_target="tpu_custom_call" | custom-call | flops 1835008 | bytes 3670016 | tf_op jit(solution)/shard_map/meridional_integral/pallas_call | solution.py:325
  24.8 0.1 collective-permute-done.1.across
  24.9 0.0 collective-permute-done.inside
  24.9 0.8 %assemble_sends.1 = bf16[16,64,128]{2,1,0:T(8,128)(2,1)} custom-call(f32[16,24,128]{2,1,0:T(8,128)S(1)} %get-tuple-element.23.combined, f32[16,8,128]{2,1,0:T(8,128)S(1)} %get-tuple-element.28.merid, f32[32,128]{1,0:T(8,128)S(1)} %collective-permute-done.inside, f32[32,128]{1,0:T(8,128)S(1)} %collective-permute-done.1.across), custom_call_target="tpu_custom_call" | custom-call | tf_op jit(solution)/shard_map/assemble_sends/pallas_call | solution.py:393
  25.7 7.7 %all-to-all-start.1 = ((bf16[16,64,128]{2,1,0:T(8,128)(2,1)}), bf16[16,64,128]{2,1,0:T(8,128)(2,1)S(1)}, u32[]{:S(2)}, u32[]{:S(2)}) async-start(bf16[16,64,128]{2,1,0:T(8,128)(2,1)} %assemble_sends.1), calls=%async_computation.1 | async-start | bytes 524288 | tf_op jit(solution)/shard_map/all_to_all | solution.py:551
  33.4 6.9 %electric_to_geo.1 = f32[2,1024]{1,0:T(2,128)} custom-call(s32[1,8]{1,0:T(1,128)S(1)} %copy-done, f32[16,16,128]{2,1,0:T(8,128)S(1)} %all-to-all-done.gathered, f32[32,128]{1,0:T(8,128)S(1)} %collective-permute-done.inside, f32[32,128]{1,0:T(8,128)S(1)} %collective-permute-done.1.across, bf16[1,1024,1024]{2,1,0:T(8,128)(2,1)S(1)} %get-tuple-element.32.held, ...), custom_call_target="tpu_custom_call" | custom-call | flops 134217728 | bytes 16777216 | tf_op jit(solution)/shard_map/electric_to_geo/pallas_call | solution.py:448
  40.4 1.1 %all-to-all-done.1.received = bf16[16,64,128]{2,1,0:T(8,128)(2,1)S(1)} async-done(((bf16[16,64,128]{2,1,0:T(8,128)(2,1)}), bf16[16,64,128]{2,1,0:T(8,128)(2,1)S(1)}, u32[]{:S(2)}, u32[]{:S(2)}) %all-to-all-start.1) | async-done | bytes 262176 | tf_op jit(solution)/shard_map/all_to_all | solution.py:551
  41.4 0.7 %stencil_source.1 = (f32[9,8,128]{2,1,0:T(8,128)}, f32[8,128]{1,0:T(8,128)}) custom-call(bf16[16,64,128]{2,1,0:T(8,128)(2,1)S(1)} %all-to-all-done.1.received), custom_call_target="tpu_custom_call" | custom-call | tf_op jit(solution)/shard_map/stencil_source/pallas_call | solution.py:507
Async XLA Ops:
  2.0 16.1 %all-to-all-start = ((f32[16,16,128]{2,1,0:T(8,128)}), f32[16,16,128]{2,1,0:T(8,128)S(1)}, u32[]{:S(2)}, u32[]{:S(2)}) async-start(f32[16,16,128]{2,1,0:T(8,128)} %pack_levels_potential.1), calls=%async_computation | async-start | bytes 262144 | tf_op jit(solution)/shard_map/all_to_all | solution.py:538
  10.0 8.1 %copy-start = (s32[1,8]{1,0:T(1,128)S(1)}, s32[1,8]{1,0:T(1,128)}, u32[]{:S(2)}) copy-start(s32[1,8]{1,0:T(1,128)} %targets.5) | copy-start | bytes 100
  10.0 8.1 %copy-start.1 = (f32[64]{0:T(128)S(1)}, f32[64]{0:T(128)}, u32[]{:S(2)}) copy-start(f32[64]{0:T(128)} %level_weights.3) | copy-start | bytes 772
  20.5 4.5 %collective-permute-start.1 = (f32[32,128]{1,0:T(8,128)S(1)}, f32[32,128]{1,0:T(8,128)S(1)}, u32[]{:S(2)}, u32[]{:S(2)}) collective-permute-start(f32[32,128]{1,0:T(8,128)S(1)} %get-tuple-element.29), channel_id=1, source_target_pairs={{0,7},{1,2},{2,1},{3,4},{4,3},{5,6},{6,5},{7,0},{8,15},{9,10},{10,... | collective-permute-start | bytes 49160 | tf_op jit(solution)/shard_map/ppermute | solution.py:524
  22.7 2.2 %collective-permute-start = (f32[32,128]{1,0:T(8,128)S(1)}, f32[32,128]{1,0:T(8,128)S(1)}, u32[]{:S(2)}, u32[]{:S(2)}) collective-permute-start(f32[32,128]{1,0:T(8,128)S(1)} %get-tuple-element.29), channel_id=1, source_target_pairs={{0,1},{1,0},{2,3},{3,2},{4,5},{5,4},{6,7},{7,6},{8,9},{9,8},{10,11... | collective-permute-start | bytes 49160 | tf_op jit(solution)/shard_map/ppermute | solution.py:524
  25.7 15.7 %all-to-all-start.1 = ((bf16[16,64,128]{2,1,0:T(8,128)(2,1)}), bf16[16,64,128]{2,1,0:T(8,128)(2,1)S(1)}, u32[]{:S(2)}, u32[]{:S(2)}) async-start(bf16[16,64,128]{2,1,0:T(8,128)(2,1)} %assemble_sends.1), calls=%async_computation.1 | async-start | bytes 524288 | tf_op jit(solution)/shard_map/all_to_all | solution.py:551
